TPU v7x, 32 devices: a whole 2x2x4 slice. The times are simulated.
32 devices in a mesh: dp: 16 (over z, y, x), mp: 2 (over core).
Axes of the slice: x: 2, y: 2, z: 4, core: 2. Of those that a mesh axis runs over, the one named last changes fastest.
Arguments:
- hidden_in: float32 [128, 198, 384], P('dp'), may hold values from -6 to 6
- keep_mask: int32 [128, 198], P('dp'), may hold values from 0 to 1, as said below
- cotangent: float32 [128, 198, 384], P('dp'), may hold values from -6 to 6
- slot_block: int32 [2, 384], replicated, may hold values from 0 to 383, each once within a row
- master: float32 [2, 2, 384, 6, 384], P('mp', None, 'dp'), may hold values from -0.375 to 0.375
- moment_one: float32 [2, 2, 384, 6, 384], P('mp', None, 'dp')
- moment_two: float32 [2, 2, 384, 6, 384], P('mp', None, 'dp'), as said below
- vector_master: float32 [2, 2, 6, 384], P('mp')
- vector_one: float32 [2, 2, 6, 384], P('mp')
- vector_two: float32 [2, 2, 6, 384], P('mp'), as said below
Outputs:
- activations: float32 [128, 198, 384], P('dp')
- input_grad: float32 [128, 198, 384], P('dp')
- matrix_grad: float32 [2, 2, 384, 6, 384], P('mp', None, 'dp')
- matrix_two: float32 [2, 2, 384, 6, 384], P('mp', None, 'dp')
- matrix_new: float32 [2, 2, 384, 6, 384], P('mp', None, 'dp')
- vector_grad: float32 [2, 2, 6, 384], P('mp')
- vector_two_new: float32 [2, 2, 6, 384], P('mp')
- vector_new: float32 [2, 2, 6, 384], P('mp')
Inputs may be any that keep to these rules, and one draw needn't show every extreme that they name: `keep_mask`: positions 0 and 1 of every image are 1; one image in every draw keeps all 198 tokens. `slot_block`: each layer's row is a permutation of the 384 blocks. `moment_two`: positive. `vector_two`: positive.
All inputs are finite; a program needn't handle non-finite values.
Results may differ from a plain program's by a relative error of at most 0.018.
Values may be sent and summed in bfloat16 or wider, within the bound.
A program may use at most 192 MiB of HBM per device.

v0:
```python
import functools

import jax
import jax.numpy as jnp
from jax import lax
from jax.experimental import pallas as pl
from jax.experimental.pallas import tpu as pltpu
from jax.sharding import PartitionSpec as P

HEADS = 6
HD = 64
FF = 1536
STEP = 10

EPS_NORM = 1e-06
BETA_ONE = 0.9
BETA_TWO = 0.999
RATE_MATRIX = 0.003
RATE_VECTOR = 0.01
DECAY_MATRIX = 0.05
EPS_ADAM = 1e-08
NEG_FILL = -1e30

F32 = jnp.float32
MESH = pl.DeviceIdType.MESH
BF16 = jnp.bfloat16


def dot_nn(left, right):
    return lax.dot_general(left, right, (((1,), (0,)), ((), ())), preferred_element_type=F32)


def dot_nt(left, right):
    return lax.dot_general(left, right, (((1,), (1,)), ((), ())), preferred_element_type=F32)


def dot_tn(left, right):
    return lax.dot_general(left, right, (((0,), (0,)), ((), ())), preferred_element_type=F32)


def fold_rows(values):
    rows, cols = values.shape
    return jnp.sum(values.reshape(rows // 8, 8, cols), 0)


def loop(count, body, unroll=True):
    lax.fori_loop(0, count, lambda i, c: (body(i), c)[1], 0, unroll=unroll)


def gelu_pair(u):
    cdf = 0.5 + 0.5 * lax.erf(u * (0.5**0.5))
    slope = cdf + u * (jnp.exp(-0.5 * u * u) * 0.3989422804014327)
    return u * cdf, slope


class Dims:
    def __init__(self, layers, images, seq, width, halves, ranks, blocks, block_rows):
        self.layers, self.images, self.seq, self.width = layers, images, seq, width
        self.halves, self.ranks, self.blocks, self.block_rows = halves, ranks, blocks, block_rows
        self.pad_seq = -(-seq // 16) * 16
        self.tokens = images * self.pad_seq
        self.slots = blocks // ranks
        side = 1
        while side**3 * 8 <= ranks:
            side *= 2
        self.axes = (ranks // (side * side), side, side)
        self.shard_rows = -(-block_rows * self.slots // 16) * 16
        self.first_rows = -(-self.shard_rows // 32) * 16
        self.groups = block_rows // 2 if 2 * self.slots % 16 == 0 else 1
        self.group = self.shard_rows // self.groups
        self.group_js = block_rows // self.groups
        self.keys = ranks * self.group
        self.half_cols = HEADS * HD // halves
        self.half_units = FF // halves
        self.natural = 4 * self.half_cols
        self.unit_blocks = self.half_units // block_rows
        self.group_units = self.group_js * self.unit_blocks
        self.half_rows = self.natural + 2 * self.half_units


def divide(values, number):
    return jnp.floor((values.astype(F32) + 0.5) * (1.0 / number))


def one_hot(rows, codes, axis):
    start, count = rows
    shape = (count, codes.shape[1]) if axis == 0 else (codes.shape[0], count)
    here = lax.broadcasted_iota(jnp.int32, shape, axis) + start
    return (here == codes.astype(jnp.int32)).astype(F32).astype(BF16)


def permute_in(dm, layer, half, s):
    cols, units = dm.half_cols, dm.half_units
    shards = [
        s.gath[layer, :, :, :, g * dm.group : (g + 1) * dm.group, :].reshape(dm.keys, dm.width)
        for g in range(dm.groups)
    ]
    code = jnp.concatenate([s.codes[layer, z] for z in range(dm.axes[0])], 1)
    for kind in range(4):
        total = None
        for g in range(dm.groups):
            part = dot_nn(one_hot((kind * cols, cols), code[g : g + 1, :], 0), shards[g])
            total = part if total is None else total + part
        total = total.astype(BF16)
        if kind < 3:
            s.w_qkv[layer, pl.ds(pl.multiple_of(kind * HEADS * HD + half * cols, 16), cols), :] = total
        else:
            s.w_out[layer, pl.ds(pl.multiple_of(half * cols, 16), cols), :] = total
    yield
    tile = min(256, dm.group_units)
    for g in range(dm.groups):
        for target, first in ((s.w_up, 0), (s.w_down, dm.group_units)):
            for start in range(0, dm.group_units, tile):
                chosen = one_hot((first + start, tile), code[dm.groups : dm.groups + 1, :], 0)
                at = pl.multiple_of(half * units + g * dm.group_units + start, 16)
                target[layer, pl.ds(at, tile), :] = dot_nn(chosen, shards[g]).astype(BF16)


def permute_out(dm, layer, half, s):
    natural, units, size = dm.natural, dm.half_units, dm.group_units

    def add(start, count):
        rows = slice(start, start + count)
        total = s.grads[half, rows, :].astype(F32) + s.grads_in[rows, :].astype(F32)
        s.grads_in[rows, :] = total.astype(BF16)

    for start in range(0, dm.half_rows, 256):
        add(start, min(256, dm.half_rows - start))
    per = dm.axes[1] * dm.axes[2] * dm.group

    def piece(z):
        codes = jnp.transpose(s.codes[layer, z])
        for g in range(dm.groups):
            up, down = natural + g * size, natural + units + g * size
            both = jnp.concatenate([s.grads_in[up : up + size, :], s.grads_in[down : down + size, :]], 0)
            rows = dot_nn(one_hot((0, natural), codes[:, g : g + 1], 1), s.grads_in[:natural, :])
            rows = rows + dot_nn(one_hot((0, 2 * size), codes[:, dm.groups : dm.groups + 1], 1), both)
            s.gath[layer, z, :, :, g * dm.group : (g + 1) * dm.group, :] = rows.astype(BF16).reshape(
                dm.axes[1], dm.axes[2], dm.group, dm.width
            )

    return piece


def prepare_codes(dm, slot_block, s):
    layers, blocks, group = dm.layers, dm.blocks, dm.group
    block = slot_block[...].astype(F32)
    high = divide(block, 16)
    zero = jnp.zeros((16 - 2 * layers, blocks), F32)
    halves = jnp.concatenate([high, block - 16.0 * high, zero], 0).astype(BF16)
    first = dm.natural // dm.block_rows
    per = dm.keys // dm.axes[0]
    size = per * max(1, 768 // per)
    for start in range(0, dm.keys, size):
        size = min(size, dm.keys - start)

        def place(shape):
            key = lax.broadcasted_iota(jnp.int32, shape, 1) + start
            rank = divide(key, group)
            inside = key.astype(F32) - rank * group
            odd = divide(inside, dm.slots)
            return rank * dm.slots + inside - odd * dm.slots, odd, inside >= dm.group_js * dm.slots

        slot, _, _ = place((blocks, size))
        same = slot == lax.broadcasted_iota(jnp.int32, (blocks, size), 0).astype(F32)
        parts = dot_nn(halves, same.astype(F32).astype(BF16))
        _, odd, padding = place((1, size))
        for layer in range(layers):
            block = 16.0 * parts[layer : layer + 1] + parts[layers + layer : layers + layer + 1]
            rows = []
            for g in range(dm.groups):
                at = block * dm.block_rows + g * dm.group_js + odd
                rows.append(jnp.where(padding | (block >= first), -1.0, at))
            inner = block - first
            at = odd * dm.unit_blocks + inner
            at = jnp.where(inner < dm.unit_blocks, at, at - dm.unit_blocks + dm.group_units)
            rows.append(jnp.where(padding | (inner < 0), -1.0, at))
            rows.append(jnp.zeros((8 - len(rows), size), F32))
            rows = jnp.concatenate(rows, 0)
            for z in range(start // per, (start + size) // per):
                s.codes[layer, z] = rows[:, z * per - start : (z + 1) * per - start]


def unit_order(dm):
    units = dm.half_units
    here = lax.broadcasted_iota(jnp.int32, (units, units), 1)
    inner = divide(here, dm.unit_blocks)
    source = (here.astype(F32) - inner * dm.unit_blocks) * dm.block_rows + inner
    same = source == lax.broadcasted_iota(jnp.int32, (units, units), 0).astype(F32)
    return same.astype(F32).astype(BF16)


def reorder(dot, row, order):
    high = row.astype(BF16)
    rest = row - high.astype(F32)
    middle = rest.astype(BF16)
    low = (rest - middle.astype(F32)).astype(BF16)
    parts = [high.astype(F32), middle.astype(F32), low.astype(F32)]
    parts.append(jnp.zeros((13, row.shape[1]), F32))
    out = dot(jnp.concatenate(parts, 0).astype(BF16), order)
    return out[0:1] + (out[1:2] + out[2:3])


def pack_vectors(dm, vectors, first, s):
    cols, units, width = dm.half_cols, dm.half_units, dm.width
    wide = HEADS * HD
    order = unit_order(dm)
    for layer in range(dm.layers):
        rows = jnp.concatenate([vectors[0, r, layer : layer + 1, :] for r in range(6)], 0)
        flat = rows[0:1]
        q, v = flat[:, :cols], flat[:, cols : 2 * cols]
        none, mid = jnp.zeros((1, cols), F32), jnp.zeros((1, wide), F32)
        tail = jnp.zeros((1, FF - 3 * wide), F32)
        zero_half = jnp.concatenate([q, none, mid, v, none, tail], 1)
        one_half = jnp.concatenate([none, q, mid, none, v, tail], 1)
        s.vec_own[layer, 0:1, :] = jnp.where(first, zero_half, one_half)
        up = reorder(dot_nn, jnp.concatenate([rows[1:2], rows[2:3]], 1), order)
        none = jnp.zeros((1, units), F32)
        s.vec_own[layer, 1:2, :] = jnp.where(
            first, jnp.concatenate([up, none], 1), jnp.concatenate([none, up], 1)
        )
        own = jnp.concatenate([rows[3:6], jnp.zeros((3, FF - width), F32)], 1)
        none = jnp.zeros((3, FF), F32)
        s.vec_own[layer, 2:5, :] = jnp.where(first, own, none)
        s.vec_own[layer, 5:8, :] = jnp.where(first, none, own)


def unpack_vectors(dm, packed, first):
    cols, units, width = dm.half_cols, dm.half_units, dm.width
    wide = HEADS * HD
    flat = packed[0:1]
    zero_half = jnp.concatenate([flat[:, :cols], flat[:, 2 * wide : 2 * wide + cols]], 1)
    one_half = jnp.concatenate([flat[:, cols : 2 * cols], flat[:, 2 * wide + cols : 3 * wide]], 1)
    flat = packed[1:2]
    up = reorder(dot_nt, jnp.where(first, flat[:, :units], flat[:, units:]), unit_order(dm))
    own = jnp.where(first, packed[2:5, :width], packed[5:8, :width])
    return jnp.concatenate(
        [
            jnp.where(first, zero_half, one_half),
            up[:, :width],
            up[:, width:],
            own,
            jnp.zeros((2, width), F32),
        ],
        0,
    )


NORM_ROWS = 208


def norm_forward(dm, layer, source, gain, shift, low_out, hat_out, devs, place):
    def chunk(i):
        rows = pl.ds(pl.multiple_of(i * NORM_ROWS, NORM_ROWS), NORM_ROWS)
        values = source[rows, :]
        centred = values - jnp.mean(values, -1, keepdims=True)
        inv = lax.rsqrt(jnp.mean(centred * centred, -1, keepdims=True) + EPS_NORM)
        hat = centred * inv
        hat_out[layer, rows, :] = hat
        devs[layer, rows, place : place + 1] = inv
        low_out[layer, rows, :] = (hat * gain + shift).astype(BF16)

    loop(dm.tokens // NORM_ROWS, chunk)


def norm_backward(dm, layer, grad, into, gain, hat_in, devs, place):
    def chunk(i, carry):
        rows = pl.ds(pl.multiple_of(i * NORM_ROWS, NORM_ROWS), NORM_ROWS)
        out, hat, inv = grad[rows, :], hat_in[layer, rows, :], devs[layer, rows, place : place + 1]
        scaled = out * gain
        first = jnp.mean(scaled, -1, keepdims=True)
        second = jnp.mean(scaled * hat, -1, keepdims=True)
        into[rows, :] = into[rows, :] + inv * (scaled - first - hat * second)
        return carry[0] + fold_rows(out * hat), carry[1] + fold_rows(out)

    zero = jnp.zeros((8, dm.width), F32)
    gains, shifts = lax.fori_loop(0, dm.tokens // NORM_ROWS, chunk, (zero, zero), unroll=True)
    return jnp.sum(gains, 0, keepdims=True), jnp.sum(shifts, 0, keepdims=True)


def lane_halves():
    lane = lax.broadcasted_iota(jnp.int32, (1, 2 * HD), 1)
    return (lane < HD).astype(F32).astype(BF16), (lane >= HD).astype(F32).astype(BF16)


def image_rows(dm, image):
    return pl.ds(pl.multiple_of(image * dm.pad_seq, 16), dm.pad_seq)


def vector_row(dm, layer, s, row, count=None):
    return s.vec[layer, row : row + 1, : count or dm.width]


def forward_norm_a(dm, layer, s):
    gain, shift = vector_row(dm, layer, s, 2), vector_row(dm, layer, s, 3)
    norm_forward(dm, layer, s.hid, gain, shift, s.low_a, s.hat_a, s.devs, 0)


def forward_project(dm, layer, s):
    wide = HEADS * HD

    def project(image):
        rows = image_rows(dm, image)
        source = s.low_a[layer, rows, :]
        for kind in range(3):
            cols = slice(kind * wide, (kind + 1) * wide)
            value = dot_nt(source, s.w_qkv[layer, cols, :]) + s.vec[layer, 0:1, cols]
            s.qkv[layer, rows, cols] = value.astype(BF16)

    loop(dm.images, project)


def forward_attend(dm, layer, s):
    wide = HEADS * HD

    halves = lane_halves()

    def attend(image):
        rows = image_rows(dm, image)
        keep = s.columns[rows, 0:1]
        for pair in range(HEADS // 2):
            cols = slice(pair * 2 * HD, (pair + 1) * 2 * HD)
            q, k, v = (s.qkv[layer, rows, n * wide + cols.start : n * wide + cols.stop] for n in range(3))
            out = None
            for side, lanes in enumerate(halves):
                scores = dot_nt(k * lanes, q)
                scores = jnp.where(keep > 0, scores * HD ** (-0.5), NEG_FILL)
                exponent = jnp.exp(scores - jnp.max(scores, 0, keepdims=True))
                probs = (exponent * (1.0 / jnp.sum(exponent, 0, keepdims=True))).astype(BF16)
                s.probs[layer, image * HEADS + 2 * pair + side] = probs
                part = dot_tn(probs, v * lanes)
                out = part if out is None else out + part
            s.att[layer, rows, cols] = out.astype(BF16)

    loop(dm.images, attend)


def forward_out(dm, layer, s):
    bias = vector_row(dm, layer, s, 4)

    def out_project(image):
        rows = image_rows(dm, image)
        s.mid[rows, :] = s.hid[rows, :] + (dot_nn(s.att[layer, rows, :], s.w_out[layer]) + bias)

    loop(dm.images, out_project)


def forward_norm_b(dm, layer, s):
    gain, shift = vector_row(dm, layer, s, 5), vector_row(dm, layer, s, 6)
    norm_forward(dm, layer, s.mid, gain, shift, s.low_b, s.hat_b, s.devs, 1)


def forward_up(dm, layer, s):
    tile = 256

    def up(image):
        rows = image_rows(dm, image)
        source = s.low_b[layer, rows, :]
        for number in range(FF // tile):
            cols = slice(number * tile, (number + 1) * tile)
            u = dot_nt(source, s.w_up[layer, cols, :]) + s.vec[layer, 1:2, cols]
            act, slope = gelu_pair(u)
            s.act[layer, rows, cols] = act.astype(BF16)
            s.slope[layer, rows, cols] = slope.astype(BF16)

    loop(dm.images, up)


def forward_down(dm, layer, s):
    bias = vector_row(dm, layer, s, 7)

    def down(image):
        rows = image_rows(dm, image)
        s.hid[rows, :] = s.mid[rows, :] + (dot_nn(s.act[layer, rows, :], s.w_down[layer]) + bias)

    loop(dm.images, down)


FORWARD = (
    ("norm", forward_norm_a),
    ("project", forward_project),
    ("attend", forward_attend),
    ("out", forward_out),
    ("mid", forward_norm_b),
    ("up", forward_up),
    ("down", forward_down),
)


def low_and_sum(dm, source, target):
    def chunk(i, carry):
        rows = pl.ds(pl.multiple_of(i * NORM_ROWS, NORM_ROWS), NORM_ROWS)
        low = source[rows, :].astype(BF16)
        target[rows, :] = low
        return carry + fold_rows(low.astype(F32))

    total = lax.fori_loop(0, dm.tokens // NORM_ROWS, chunk, jnp.zeros((8, dm.width), F32), unroll=True)
    return jnp.sum(total, 0, keepdims=True)


def column_sums(dm, read, cols):
    def chunk(i, carry):
        rows = pl.ds(pl.multiple_of(i * NORM_ROWS, NORM_ROWS), NORM_ROWS)
        return carry + fold_rows(read(rows).astype(F32))

    total = lax.fori_loop(0, dm.tokens // NORM_ROWS, chunk, jnp.zeros((8, cols), F32), unroll=True)
    return jnp.sum(total, 0, keepdims=True)


def backward_start(dm, layer, s):
    s.vec_grad[layer, 7:8, : dm.width] = low_and_sum(dm, s.hid, s.low_g)


def backward_units(dm, layer, s):
    tile, units = 256, dm.half_units
    per_half = units // tile

    def unit_tile(number):
        cols = pl.ds(pl.multiple_of(number * tile, tile), tile)
        grad = dot_nt(s.low_g[...], s.w_down[layer, cols, :])
        grad = (grad * s.slope[layer, :, cols].astype(F32)).astype(BF16)
        s.slope[layer, :, cols] = grad
        half, at = number // per_half, pl.multiple_of((number % per_half) * tile, tile)
        s.grads[half, pl.ds(dm.natural + units + at, tile), :] = dot_tn(
            s.act[layer, :, cols], s.low_g[...]
        ).astype(BF16)
        s.grads[half, pl.ds(dm.natural + at, tile), :] = dot_tn(grad, s.low_b[layer]).astype(BF16)

    loop(FF // tile, unit_tile)


def backward_up_sums(dm, layer, s):
    s.vec_grad[layer, 1:2, :] = column_sums(dm, lambda rows: s.slope[layer, rows, :], FF)


def backward_down(dm, layer, s):
    def down(image):
        rows = image_rows(dm, image)
        s.mid[rows, :] = dot_nn(s.slope[layer, rows, :], s.w_up[layer])

    loop(dm.images, down)


def backward_norm_b(dm, layer, s):
    width = dm.width
    gain = vector_row(dm, layer, s, 5)
    gains, shifts = norm_backward(dm, layer, s.mid, s.hid, gain, s.hat_b, s.devs, 1)
    s.vec_grad[layer, 5:6, :width] = gains
    s.vec_grad[layer, 6:7, :width] = shifts
    s.vec_grad[layer, 4:5, :width] = low_and_sum(dm, s.hid, s.low_g)


def backward_out(dm, layer, s):
    cols = dm.half_cols
    value = dot_tn(s.att[layer], s.low_g[...]).astype(BF16)
    for half in range(dm.halves):
        s.grads[half, 3 * cols : dm.natural, :] = value[half * cols : (half + 1) * cols]

    def out_project(image):
        rows = image_rows(dm, image)
        s.att[layer, rows, :] = dot_nt(s.low_g[rows, :], s.w_out[layer]).astype(BF16)

    loop(dm.images, out_project)


def backward_attend(dm, layer, s, part):
    wide = HEADS * HD
    half = dm.images // 2

    halves = lane_halves()

    def attend(image):
        rows = image_rows(dm, image)
        keep = s.columns[rows, 0:1] * HD ** (-0.5)
        for pair in range(HEADS // 2):
            cols = slice(pair * 2 * HD, (pair + 1) * 2 * HD)
            q, k, v = (s.qkv[layer, rows, n * wide + cols.start : n * wide + cols.stop] for n in range(3))
            out = s.att[layer, rows, cols]
            parts = None
            for side, lanes in enumerate(halves):
                probs = s.probs[layer, image * HEADS + 2 * pair + side]
                grad = dot_nt(v * lanes, out)
                wide_probs = probs.astype(F32)
                total = jnp.sum(wide_probs * grad, 0, keepdims=True)
                raw = (wide_probs * (grad - total) * keep).astype(BF16)
                found = dot_tn(raw, k * lanes), dot_nn(raw, q * lanes), dot_nn(probs, out * lanes)
                parts = found if parts is None else [p + f for p, f in zip(parts, found)]
            for n, part in enumerate(parts):
                s.qkv[layer, rows, n * wide + cols.start : n * wide + cols.stop] = part.astype(BF16)

    loop(half, lambda i: attend(part * half + i))


def backward_rows(dm, layer, s):
    wide, cols = HEADS * HD, dm.half_cols
    for kind in range(3):
        value = dot_tn(s.qkv[layer, :, kind * wide : (kind + 1) * wide], s.low_a[layer]).astype(BF16)
        for half in range(dm.halves):
            s.grads[half, kind * cols : (kind + 1) * cols, :] = value[half * cols : (half + 1) * cols]


def backward_sums(dm, layer, s):
    wide = 3 * HEADS * HD
    s.vec_grad[layer, 0:1, :wide] = column_sums(dm, lambda rows: s.qkv[layer, rows, :], wide)


def backward_project(dm, layer, s):
    def project(image):
        rows = image_rows(dm, image)
        s.mid[rows, :] = dot_nn(s.qkv[layer, rows, :], s.w_qkv[layer])

    loop(dm.images, project)


def backward_norm_a(dm, layer, s):
    width = dm.width
    gain = vector_row(dm, layer, s, 2)
    gains, shifts = norm_backward(dm, layer, s.mid, s.hid, gain, s.hat_a, s.devs, 0)
    s.vec_grad[layer, 2:3, :width] = gains
    s.vec_grad[layer, 3:4, :width] = shifts


BACKWARD = (
    ("start", backward_start),
    ("units", backward_units),
    ("sums", backward_up_sums),
    ("down", backward_down),
    ("mid", backward_norm_b),
    ("out", backward_out),
    ("attend", functools.partial(backward_attend, part=0)),
    ("attended", functools.partial(backward_attend, part=1)),
    ("rows", backward_rows),
    ("more", backward_sums),
    ("project", backward_project),
    ("end", backward_norm_a),
)


class Net:
    def __init__(self, dm, s):
        self.dm, self.s, self.keys = dm, s, {}
        self.rank, self.core = lax.axis_index("dp"), lax.axis_index("mp")
        _, rows, cols = dm.axes
        self.place = (self.rank // (rows * cols), (self.rank // cols) % rows, self.rank % cols)

    def device(self, *offsets):
        z, y, x = ((here + o) % size for here, o, size in zip(self.place, offsets, self.dm.axes))
        return ((z * self.dm.axes[1] + y) * self.dm.axes[2] + x, self.core)

    def sibling(self):
        return (self.rank, 1 - self.core)

    def on_axis(self, axis, offset):
        return self.device(*(offset if axis == k else 0 for k in range(3)))

    def along(self, axis, offset):
        return (self.place[axis] + offset) % self.dm.axes[axis]

    def partners(self):
        depth = self.dm.axes[0]
        found = [self.sibling()]
        found += [self.device(o, 0, 0) for o in range(1, depth)]
        return found + [self.device(0, *o) for o in self.plane()]

    def plane(self):
        _, rows, cols = self.dm.axes
        return [(p, q) for p in range(rows) for q in range(cols) if p or q]

    def greet(self, semaphore):
        for partner in self.partners():
            pl.semaphore_signal(semaphore, inc=1, device_id=partner, device_id_type=MESH)

    def met(self, semaphore):
        pl.semaphore_wait(semaphore, len(self.partners()))

    def copy(self, key, layer, source, target, device):
        name, count, index = key
        if name not in self.keys:
            used = sum(n for _, n in self.keys.values()) * self.dm.layers
            self.keys[name] = (used, count)
        first, known = self.keys[name]
        assert known == count
        number = first + layer * count + index
        return pltpu.make_async_remote_copy(
            src_ref=source,
            dst_ref=target,
            send_sem=self.s.send_sems.at[number],
            recv_sem=self.s.recv_sems.at[number],
            device_id=device,
            device_id_type=MESH,
        )


def copies_needed(dm):
    depth, rows, cols = dm.axes
    cross = depth * (cols + rows - 2)
    vectors = 1 + (depth - 1) + (rows * cols - 1)
    return dm.layers * (depth - 1 + 2 * cross + 6 + 2 + vectors + 1 + 2 * dm.images)


def start_all(copies):
    for copy in copies:
        copy.start()


def wait_all(copies):
    for copy in copies:
        copy.wait()


class Gather:
    def __init__(self, dm, net, s, layer):
        self.dm, self.net, self.layer, self.buf = dm, net, layer, s.gath.at[layer]
        self.head = pl.ds(0, dm.first_rows)
        self.tail = pl.ds(dm.first_rows, dm.shard_rows - dm.first_rows)
        depth = dm.axes[0]
        self.order = sorted(range(1, depth), key=lambda o: min(o, depth - o))

    def keys(self, name, piece, number):
        _, rows, cols = self.dm.axes
        count = rows + cols - 2
        return (name, self.dm.axes[0] * count, piece * count + number)

    def one(self, offset):
        ref = self.buf.at[self.net.place]
        key = ("one", self.dm.axes[0] - 1, offset - 1)
        return [self.net.copy(key, self.layer, ref, ref, self.net.on_axis(0, offset))]

    def pairs(self, name, piece, pairs):
        copies = []
        for ref, axis in pairs:
            for o in range(1, self.dm.axes[axis]):
                key = self.keys(name, piece, len(copies))
                copies.append(self.net.copy(key, self.layer, ref, ref, self.net.on_axis(axis, o)))
        return copies

    def two(self, piece):
        at, (_, y, x) = self.net.along(0, -piece), self.net.place
        return self.pairs(
            "two", piece, [(self.buf.at[at, y, x, self.head], 2), (self.buf.at[at, y, x, self.tail], 1)]
        )

    def three(self, piece):
        at, (_, y, x) = self.net.along(0, -piece), self.net.place
        return self.pairs(
            "three", piece, [(self.buf.at[at, y, :, self.head], 1), (self.buf.at[at, :, x, self.tail], 2)]
        )

    def begin(self):
        for offset in range(1, self.dm.axes[0]):
            start_all(self.one(offset))
        start_all(self.two(0))

    def steps(self):
        found = []
        before = 0
        for piece in self.order + [None]:

            def step(before=before, piece=piece):
                if piece is not None:
                    wait_all(self.one(piece))
                    start_all(self.two(piece))
                wait_all(self.two(before))
                start_all(self.three(before))

            found.append(step)
            before = piece
        return found

    def end(self):
        for piece in range(self.dm.axes[0]):
            wait_all(self.three(piece))


class Scatter:
    def __init__(self, dm, net, s, layer):
        self.dm, self.net, self.s, self.layer, self.buf = dm, net, s, layer, s.gath.at[layer]
        self.head = pl.ds(0, dm.first_rows)
        self.tail = pl.ds(dm.first_rows, dm.shard_rows - dm.first_rows)

    def pairs(self, name, piece, parts):
        copies = []
        _, rows, cols = self.dm.axes
        count = rows + cols - 2
        for axis, make in parts:
            for o in range(1, self.dm.axes[axis]):
                key = (name, self.dm.axes[0] * count, piece * count + len(copies))
                source, target = make(self.net.along(axis, o), o - 1)
                copies.append(self.net.copy(key, 0, source, target, self.net.on_axis(axis, o)))
        return copies

    def one(self, piece):
        at, s, buf = self.net.along(0, piece), self.s, self.buf
        return self.pairs(
            "three",
            piece,
            [
                (1, lambda to, n: (buf.at[at, to, :, self.head], s.one_a.at[piece, n])),
                (2, lambda to, n: (buf.at[at, :, to, self.tail], s.one_b.at[piece, n])),
            ],
        )

    def two(self, piece):
        at, s, buf, (_, y, x) = self.net.along(0, piece), self.s, self.buf, self.net.place
        return self.pairs(
            "two",
            piece,
            [
                (2, lambda to, n: (buf.at[at, y, to, self.head], s.two_a.at[piece, n])),
                (1, lambda to, n: (buf.at[at, to, x, self.tail], s.two_b.at[piece, n])),
            ],
        )

    def three(self, piece):
        _, y, x = self.net.place
        source = self.buf.at[self.net.along(0, piece), y, x]
        target = self.s.three.at[self.layer, piece - 1]
        key = ("one", self.dm.axes[0] - 1, piece - 1)
        turn = self.dm.layers - 1 - self.layer
        return self.net.copy(key, turn, source, target, self.net.device(piece, 0, 0))

    def add(self, at, parts):
        value = self.buf[at].astype(F32)
        for part in parts:
            value = value + part.astype(F32)
        self.buf[at] = value.astype(BF16)

    def second(self, piece):
        _, rows, cols = self.dm.axes
        at, s, (_, y, x) = self.net.along(0, piece), self.s, self.net.place
        wait_all(self.one(piece))
        self.add((at, y, slice(None), self.head), [s.one_a[piece, o] for o in range(rows - 1)])
        self.add((at, slice(None), x, self.tail), [s.one_b[piece, o] for o in range(cols - 1)])
        start_all(self.two(piece))

    def third(self, piece):
        _, rows, cols = self.dm.axes
        at, s, (_, y, x) = self.net.along(0, piece), self.s, self.net.place
        wait_all(self.two(piece))
        self.add((at, y, x, self.head), [s.two_a[piece, o] for o in range(cols - 1)])
        self.add((at, y, x, self.tail), [s.two_b[piece, o] for o in range(rows - 1)])

        @pl.when(piece > 0)
        def _():
            self.three(piece).start()

    def end(self):
        value = self.buf[self.net.place].astype(F32)
        for piece in range(1, self.dm.axes[0]):
            self.three(piece).wait()
            value = value + self.s.three[self.layer, piece - 1].astype(F32)
        return value


class Totals:
    def __init__(self, dm, net, s, layer, first):
        self.dm, self.net, self.s, self.layer, self.first = dm, net, s, layer, first

    def across(self):
        s, layer = self.s, self.layer
        copy = self.net.copy(
            ("cores", 1, 0), layer, s.vec_grad.at[layer], s.vec_back.at[layer], self.net.sibling()
        )
        return [copy]

    def plane(self):
        _, y, x = self.net.place
        here = self.s.vec_p.at[self.layer, y * self.dm.axes[2] + x]
        offsets = self.net.plane()
        return [
            self.net.copy(("plane", len(offsets), n), self.layer, here, here, self.net.device(0, *o))
            for n, o in enumerate(offsets)
        ]

    def depth(self):
        here = self.s.vec_z.at[self.layer, self.net.place[0]]
        size = self.dm.axes[0]
        return [
            self.net.copy(("depth", size - 1, o - 1), self.layer, here, here, self.net.on_axis(0, o))
            for o in range(1, size)
        ]

    def begin(self):
        start_all(self.across())

    def second(self):
        s, layer, (_, y, x) = self.s, self.layer, self.net.place
        wait_all(self.across())
        value = unpack_vectors(self.dm, s.vec_grad[layer] + s.vec_back[layer], self.first)
        s.vec_p[layer, y * self.dm.axes[2] + x] = value
        start_all(self.plane())

    def third(self):
        s, layer = self.s, self.layer
        wait_all(self.plane())
        value = s.vec_p[layer, 0]
        for o in range(1, self.dm.axes[1] * self.dm.axes[2]):
            value = value + s.vec_p[layer, o]
        s.vec_z[layer, self.net.place[0]] = value
        start_all(self.depth())

    def end(self):
        wait_all(self.depth())
        value = self.s.vec_z[self.layer, 0]
        for o in range(1, self.dm.axes[0]):
            value = value + self.s.vec_z[self.layer, o]
        return value


class Refs:
    pass


def scratch_shapes(dm):
    layers, tokens, width, wide = dm.layers, dm.tokens, dm.width, HEADS * HD
    depth, rows, cols = dm.axes
    head, tail = dm.first_rows, dm.shard_rows - dm.first_rows
    vmem, copies = pltpu.VMEM, copies_needed(dm)
    return dict(
        hid=vmem((tokens, width), F32),
        mid=vmem((tokens, width), F32),
        columns=vmem((tokens, 8), F32),
        devs=vmem((layers, tokens, 8), F32),
        low_a=vmem((layers, tokens, width), BF16),
        low_b=vmem((layers, tokens, width), BF16),
        low_g=vmem((tokens, width), BF16),
        hat_a=vmem((layers, tokens, width), F32),
        hat_b=vmem((layers, tokens, width), F32),
        qkv=vmem((layers, tokens, 3 * wide), BF16),
        probs=vmem((layers, dm.images * HEADS, dm.pad_seq, dm.pad_seq), BF16),
        att=vmem((layers, tokens, wide), BF16),
        act=vmem((layers, tokens, FF), BF16),
        slope=vmem((layers, tokens, FF), BF16),
        w_qkv=vmem((layers, 3 * wide, width), BF16),
        w_out=vmem((layers, wide, width), BF16),
        w_up=vmem((layers, FF, width), BF16),
        w_down=vmem((layers, FF, width), BF16),
        grads=vmem((dm.halves, dm.half_rows, width), BF16),
        grads_in=vmem((dm.half_rows, width), BF16),
        gath=vmem((layers, depth, rows, cols, dm.shard_rows, width), BF16),
        one_a=vmem((depth, rows - 1, cols, head, width), BF16),
        one_b=vmem((depth, cols - 1, rows, tail, width), BF16),
        two_a=vmem((depth, cols - 1, head, width), BF16),
        two_b=vmem((depth, rows - 1, tail, width), BF16),
        three=vmem((layers, depth - 1, dm.shard_rows, width), BF16),
        rows=vmem((dm.shard_rows, width), F32),
        tok_in=vmem((dm.images, dm.seq, width), F32),
        tok_out=vmem((dm.images, dm.seq, width), F32),
        codes=vmem((layers, depth, 8, dm.keys // depth), F32),
        vec_own=vmem((layers, 8, FF), F32),
        vec=vmem((layers, 8, FF), F32),
        vec_grad=vmem((layers, 8, FF), F32),
        vec_in=vmem((layers, 8, FF), F32),
        vec_back=vmem((layers, 8, FF), F32),
        vec_z=vmem((layers, depth, 8, width), F32),
        vec_p=vmem((layers, rows * cols, 8, width), F32),
        vec_sum=vmem((layers, 8, width), F32),
        keep_row=vmem((8, -(-dm.pad_seq // 128) * 128), F32),
        send_sems=pltpu.SemaphoreType.DMA((copies,)),
        recv_sems=pltpu.SemaphoreType.DMA((copies,)),
        load_sems=pltpu.SemaphoreType.DMA((dm.images,)),
        store_sems=pltpu.SemaphoreType.DMA((dm.images,)),
        credit=pltpu.SemaphoreType.REGULAR,
        core_credit=pltpu.SemaphoreType.REGULAR,
    )


def load_tokens(dm, source, target, scale=None):
    tail = dm.pad_seq - 16
    for image in range(dm.images):
        start = image * dm.pad_seq
        target[start + tail : start + dm.pad_seq, :] = jnp.zeros((16, dm.width), F32)
        value = source[image]
        if scale is not None:
            value = value * scale[start : start + dm.seq, 0:1]
        target[start : start + dm.seq, :] = value


class Tokens:
    def __init__(self, dm, net, s):
        self.dm, self.net, self.s = dm, net, s

    def image(self, ref, number):
        return ref.at[:, self.net.core * self.dm.images + number]

    def load(self, ref):
        sems = self.s.load_sems
        return [
            pltpu.make_async_copy(self.image(ref, i), self.s.tok_in.at[i], sems.at[i])
            for i in range(self.dm.images)
        ]

    def store(self, ref, turn):
        copies = []
        for i in range(self.dm.images):
            source, target = self.s.tok_out.at[i], self.image(ref, i)
            copies.append(pltpu.make_async_copy(source, target, self.s.store_sems.at[i]))
            key = ("tokens", self.dm.images, i)
            copies.append(self.net.copy(key, turn, source, target, self.net.sibling()))
        return copies


def prepare_keep(dm, keep_mask, first, s):
    kept = keep_mask[...].astype(F32)
    kept = jnp.where(first, kept[: dm.images], kept[dm.images :])
    s.keep_row[...] = jnp.zeros(s.keep_row.shape, F32)
    s.keep_row[: dm.images, : dm.seq] = kept
    columns = jnp.transpose(s.keep_row[...])
    for image in range(dm.images):
        rows = slice(image * dm.pad_seq, (image + 1) * dm.pad_seq)
        s.columns[rows, 0:1] = columns[: dm.pad_seq, image : image + 1]


def own_shard(dm, master, net, s):
    z, y, x = net.place
    if dm.shard_rows > dm.block_rows * dm.slots:
        s.rows[...] = jnp.zeros(s.rows.shape, F32)
    for layer in range(dm.layers):
        for j in range(dm.block_rows):
            s.rows[j * dm.slots : (j + 1) * dm.slots, :] = master[0, layer, j]
        s.gath[layer, z, y, x] = s.rows[...].astype(BF16)


def step_kernel(dm, names, hidden, keep_mask, cotangent, slot_block, master, vectors, acts, grad_in, matrix, vec_out, *scratch):
    s = Refs()
    for name, ref in zip(names, scratch):
        setattr(s, name, ref)
    net = Net(dm, s)
    first = net.core == 0
    tokens = Tokens(dm, net, s)
    cols, units, depth = dm.half_cols, dm.half_units, dm.axes[0]
    assert dm.layers == 2
    gathers = [Gather(dm, net, s, layer) for layer in range(dm.layers)]
    barrier = pltpu.get_barrier_semaphore()
    net.greet(barrier)
    start_all(tokens.load(hidden))
    own_shard(dm, master, net, s)
    net.met(barrier)
    gathers[0].begin()
    pack_vectors(dm, vectors, first, s)
    other_vec = net.copy(("vectors", 1, 0), 0, s.vec_own, s.vec_in, net.sibling())
    other_vec.start()
    prepare_codes(dm, slot_block, s)
    prepare_keep(dm, keep_mask, first, s)
    wait_all(tokens.load(hidden))
    load_tokens(dm, s.tok_in, s.hid)
    start_all(tokens.load(cotangent))
    other_vec.wait()
    s.vec[...] = s.vec_own[...] + s.vec_in[...]
    for step in gathers[0].steps():
        step()
    gathers[1].begin()
    steps = gathers[1].steps()

    def weights(layer):
        parts = [(s.w_qkv, kind * HEADS * HD + net.core * cols, cols) for kind in range(3)]
        parts += [(s.w_out, net.core * cols, cols), (s.w_up, net.core * units, units)]
        parts.append((s.w_down, net.core * units, units))
        copies = []
        for ref, start, count in parts:
            rows = ref.at[layer, pl.ds(pl.multiple_of(start, 16), count)]
            key = ("weights", len(parts), len(copies))
            copies.append(net.copy(key, layer, rows, rows, net.sibling()))
        return copies

    def forward(layer):
        shares = weights(layer)
        for name, phase in FORWARD:
            phase(dm, layer, s)
            if name == "norm":
                Gather(dm, net, s, layer).end()
                parts = permute_in(dm, layer, net.core, s)
                next(parts)
                start_all(shares[:4])
                next(parts, None)
                start_all(shares[4:])
                wait_all(shares[:3])
            if name == "attend":
                shares[3].wait()
            if name == "mid":
                shares[4].wait()
            if name == "up":
                shares[5].wait()
            if name in ("norm", "project", "attend", "mid"):
                now = [steps.pop(0)]
                if name == "mid":
                    now, steps[:] = now + steps, []

                @pl.when(layer + 1 < dm.layers)
                def _(now=now):
                    for step in now:
                        step()

    lax.fori_loop(0, dm.layers, lambda i, c: (forward(i), c)[1], 0)
    for image in range(dm.images):
        rows = slice(image * dm.pad_seq, image * dm.pad_seq + dm.seq)
        s.tok_out[image] = s.hid[rows, :] * s.columns[rows, 0:1]
    start_all(tokens.store(acts, 0))
    wait_all(tokens.load(cotangent))
    load_tokens(dm, s.tok_in, s.hid, s.columns)

    def put_rows(layer):
        s.rows[...] = Scatter(dm, net, s, layer).end()
        for j in range(dm.block_rows):
            matrix[0, layer, j] = s.rows[j * dm.slots : (j + 1) * dm.slots, :]

    def put_vectors(layer):
        value = Totals(dm, net, s, layer, first).end()
        for r in range(vec_out.shape[1]):
            vec_out[0, r, layer : layer + 1, :] = value[r : r + 1]

    def share(layer, number):
        rows = (pl.ds(dm.natural, 2 * units), pl.ds(0, dm.natural))[number]
        source = s.grads.at[1 - net.core, rows]
        return net.copy(("shares", 2, number), layer, source, s.grads_in.at[rows], net.sibling())

    def backward(turn):
        layer = dm.layers - 1 - turn
        later = turn > 0
        before = Scatter(dm, net, s, 1)
        totals_before = Totals(dm, net, s, 1, first)

        def when_later(body, *args):
            pl.when(later)(lambda: body(*args))

        order = list(range(depth - 1, -1, -1))
        for name, phase in BACKWARD:
            phase(dm, layer, s)
            if name == "start":
                when_later(totals_before.second)
            if name == "units":
                when_later(pl.semaphore_wait, s.core_credit, 1)
                share(layer, 0).start()
            if name in ("units", "down", "mid", "out"):
                count = -(-depth // 4)
                now, order = order[:count], order[count:]
                for piece in now:
                    when_later(before.second, piece)
            if name == "out":
                order = list(range(depth - 1, -1, -1))
            if name in ("attend", "attended"):
                count = depth // 2
                now, order = order[:count], order[count:]
                for piece in now:
                    when_later(before.third, piece)
            if name == "attended":
                when_later(net.greet, s.credit)
                when_later(totals_before.third)
            if name == "rows":
                share(layer, 1).start()
            if name == "more":
                wait_all([share(layer, 0), share(layer, 1)])
                fill = permute_out(dm, layer, net.core, s)
                when_later(net.met, s.credit)
                scatter = Scatter(dm, net, s, layer)

                def piece_out(number, carry):
                    piece = depth - 1 - number
                    fill(net.along(0, piece))
                    start_all(scatter.one(piece))
                    return carry

                lax.fori_loop(0, depth, piece_out, 0)

                @pl.when(layer > 0)
                def _():
                    pl.semaphore_signal(
                        s.core_credit, inc=1, device_id=net.sibling(), device_id_type=MESH
                    )
        Totals(dm, net, s, layer, first).begin()

    lax.fori_loop(0, dm.layers, lambda i, c: (backward(i), c)[1], 0)
    wait_all(tokens.store(acts, 0))
    for image in range(dm.images):
        rows = slice(image * dm.pad_seq, image * dm.pad_seq + dm.seq)
        s.tok_out[image] = s.hid[rows, :]
    start_all(tokens.store(grad_in, 1))
    scatter, totals = Scatter(dm, net, s, 0), Totals(dm, net, s, 0, first)
    totals.second()
    loop(depth, lambda n: scatter.second(depth - 1 - n))
    put_vectors(1)
    put_rows(1)
    totals.third()
    loop(depth, lambda n: scatter.third(depth - 1 - n))
    put_vectors(0)
    put_rows(0)
    wait_all(tokens.store(grad_in, 1))


def run_step(dm, hidden_in, keep_mask, cotangent, slot_block, master, vector_master):
    shapes = scratch_shapes(dm)
    out_shape = (
        jax.ShapeDtypeStruct(hidden_in.shape, F32),
        jax.ShapeDtypeStruct(hidden_in.shape, F32),
        jax.ShapeDtypeStruct(master.shape, F32),
        jax.ShapeDtypeStruct(vector_master.shape, F32),
    )
    full, far = pl.BlockSpec(memory_space=pltpu.VMEM), pl.BlockSpec(memory_space=pl.ANY)
    return pl.pallas_call(
        functools.partial(step_kernel, dm, tuple(shapes)),
        out_shape=out_shape,
        in_specs=[far, full, far, full, full, full],
        out_specs=[far, far, full, full],
        scratch_shapes=list(shapes.values()),
        compiler_params=pltpu.CompilerParams(
            vmem_limit_bytes=63 * 2**20, collective_id=0, has_side_effects=True
        ),
    )(hidden_in, keep_mask, cotangent, slot_block, master, vector_master)


def adam_step(weight, grad_sum, first_old, second_old, rate, decay):
    first_new = BETA_ONE * first_old + (1.0 - BETA_ONE) * grad_sum
    second_new = BETA_TWO * second_old + (1.0 - BETA_TWO) * grad_sum * grad_sum
    first_hat = first_new / (1.0 - BETA_ONE**STEP)
    second_hat = second_new / (1.0 - BETA_TWO**STEP)
    return (
        second_new,
        weight - rate * (first_hat / (jnp.sqrt(second_hat) + EPS_ADAM) + decay * weight),
    )


def finish_kernel(parts, *refs):
    large, matrix, vector = refs[:2], refs[2:6], refs[6:10]
    large_out, matrix_out, vector_out = refs[10:12], refs[12:15], refs[15:18]
    stage, matrix_in, vector_in, matrix_done, vector_done, stage_sems, load_sems, store_sems = refs[18:]
    loads, stores = [], []
    rows_all = stage.shape[1]
    size = -(-rows_all // parts)
    for start in range(0, rows_all, size):
        for number, (source, target) in enumerate(zip(large, large_out)):
            rows = pl.ds(start, min(size, rows_all - start))
            held, sem = stage.at[number, rows], stage_sems.at[len(loads)]
            loads.append(pltpu.make_async_copy(source.at[rows], held, sem))
            stores.append(pltpu.make_async_copy(held, target.at[rows], sem))
    matrix_loads = [
        pltpu.make_async_copy(ref, matrix_in.at[n], load_sems.at[n]) for n, ref in enumerate(matrix)
    ]
    vector_loads = [
        pltpu.make_async_copy(ref, vector_in.at[n], load_sems.at[4 + n]) for n, ref in enumerate(vector)
    ]
    results = [
        pltpu.make_async_copy(matrix_done.at[n], ref, store_sems.at[n])
        for n, ref in enumerate(matrix_out)
    ]
    results += [
        pltpu.make_async_copy(vector_done.at[n], ref, store_sems.at[3 + n])
        for n, ref in enumerate(vector_out)
    ]
    start_all(vector_loads + matrix_loads + loads)
    wait_all(vector_loads + matrix_loads)

    def adam(held, done, at, rate, decay):
        grad, weight, one, two = (held[(n, *at)] for n in range(4))
        done[(0, *at)] = grad
        done[(1, *at)], done[(2, *at)] = adam_step(weight, grad, one, two, rate, decay)

    for layer in range(matrix_in.shape[2]):
        adam(matrix_in, matrix_done, (0, layer), RATE_MATRIX, DECAY_MATRIX)
    adam(vector_in, vector_done, (0,), RATE_VECTOR, 0.0)
    start_all(results)
    for load, store in zip(loads, stores):
        load.wait()
        store.start()
    wait_all(stores + results)


def run_finish(acts, grad_in, matrix, vector):
    parts = 1
    far = pl.BlockSpec(memory_space=pl.ANY)
    shapes = [acts, grad_in] + [matrix[0]] * 3 + [vector[0]] * 3
    return pl.pallas_call(
        functools.partial(finish_kernel, parts),
        out_shape=tuple(jax.ShapeDtypeStruct(a.shape, F32) for a in shapes),
        in_specs=[far] * 10,
        out_specs=[far] * 8,
        scratch_shapes=[
            pltpu.VMEM((2, *acts.shape), F32),
            pltpu.VMEM((4, *matrix[0].shape), F32),
            pltpu.VMEM((4, *vector[0].shape), F32),
            pltpu.VMEM((3, *matrix[0].shape), F32),
            pltpu.VMEM((3, *vector[0].shape), F32),
            pltpu.SemaphoreType.DMA((2 * parts,)),
            pltpu.SemaphoreType.DMA((8,)),
            pltpu.SemaphoreType.DMA((6,)),
        ],
        compiler_params=pltpu.CompilerParams(vmem_limit_bytes=63 * 2**20),
    )(acts, grad_in, *matrix, *vector)


def shards(
    hidden_in, keep_mask, cotangent, slot_block, master, moment_one, moment_two, vector_master, vector_one, vector_two
):
    images, seq, width = hidden_in.shape
    halves, ranks = lax.axis_size("mp"), lax.axis_size("dp")
    dm = Dims(
        master.shape[1], images // halves, seq, width, halves, ranks, slot_block.shape[1], master.shape[3]
    )
    matrix = [array.swapaxes(2, 3) for array in (master, moment_one, moment_two)]
    vector = [array.swapaxes(1, 2) for array in (vector_master, vector_one, vector_two)]
    acts, grad_in, matrix_grad, vector_grad = run_step(
        dm, hidden_in.swapaxes(0, 1), keep_mask, cotangent.swapaxes(0, 1), slot_block, matrix[0], vector[0]
    )
    results = run_finish(acts, grad_in, [matrix_grad] + matrix, [vector_grad] + vector)
    return tuple(
        array.swapaxes(*axes)
        for array, axes in zip(results, [(0, 1)] * 2 + [(2, 3)] * 3 + [(1, 2)] * 3)
    )


def solution(mesh):
    images, rows, copied = P("dp", None, None), P("mp", None, "dp", None, None), P("mp", None, None, None)
    return jax.shard_map(
        shards,
        mesh=mesh,
        in_specs=(images, P("dp", None), images, P(), rows, rows, rows, copied, copied, copied),
        out_specs=(images, images, rows, rows, rows, copied, copied, copied),
        check_vma=False,
    )
```

profile of v0, /device:TPU:0, one launch (start us, length us, event | category | flops | bytes accessed | tf_op | source)
XLA Modules:
  0.0 141.8 jit_solution(12724585085427407704)
XLA Ops:
  0.6 135.5 %shard_map.161 = (f32[198,8,384]{2,1,0:T(8,128)}, f32[198,8,384]{2,1,0:T(8,128)}, f32[1,2,6,24,384]{4,3,2,1,0:T(8,128)}, f32[1,6,2,384]{3,2,1,0:T(2,128)}) custom-call(f32[198,8,384]{2,1,0:T(8,128)} %bitcast.16, s32[8,198]{1,0:T(8,128)} %keep_mask.1, f32[198,8,384]{2,1,0:T(8,128)} %bitcast.17, s32[2,384]{1,0:T(2,128)} %slot_block.1, ...), custom_call_target="tpu_custom_call" | custom-call | tf_op jit(solution)/shard_map/pallas_call | solution.py:1099
  136.1 5.5 %shard_map.162 = (f32[198,8,384]{2,1,0:T(8,128)}, f32[198,8,384]{2,1,0:T(8,128)}, f32[1,2,6,24,384]{4,3,2,1,0:T(8,128)}, f32[1,2,6,24,384]{4,3,2,1,0:T(8,128)}, ...) custom-call(f32[198,8,384]{2,1,0:T(8,128)} %get-tuple-element.20.ref, ...), custom_call_target="tpu_custom_call" | custom-call | tf_op jit(solution)/shard_map/pallas_call | solution.py:1171
where the time goes:
time: 142 us
  Pallas kernels  141 us (99%)
    pallas_call x1, Pallas kernels, run_step(): pl.pallas_call(functools.partial(step_kernel, dm, tuple(shapes)), out_sha...  135 us
    pallas_call x1, Pallas kernels, run_finish(): pl.pallas_call(functools.partial(finish_kernel, parts), out_shape=tuple((...  5.52 us

commit v1 on v0

--- a/solution.py
+++ b/solution.py
@@ -65,7 +65,9 @@
             side *= 2
         self.axes = (ranks // (side * side), side, side)
         self.shard_rows = -(-block_rows * self.slots // 16) * 16
-        self.first_rows = -(-self.shard_rows // 32) * 16
+        self.last_rows = 16 * (self.shard_rows // 144)
+        self.most_rows = self.shard_rows - self.last_rows
+        self.first_rows = -(-self.most_rows // 32) * 16
         self.groups = block_rows // 2 if 2 * self.slots % 16 == 0 else 1
         self.group = self.shard_rows // self.groups
         self.group_js = block_rows // self.groups
@@ -74,8 +76,8 @@
         self.half_units = FF // halves
         self.natural = 4 * self.half_cols
         self.unit_blocks = self.half_units // block_rows
-        self.group_units = self.group_js * self.unit_blocks
-        self.half_rows = self.natural + 2 * self.half_units
+        self.kind_blocks = self.half_cols // block_rows
+        self.first_unit = 4 * self.kind_blocks
 
 
 def divide(values, number):
@@ -90,56 +92,68 @@
 
 
 def permute_in(dm, layer, half, s):
-    cols, units = dm.half_cols, dm.half_units
+    cols, units, some = dm.half_cols, dm.half_units, dm.unit_blocks
     shards = [
         s.gath[layer, :, :, :, g * dm.group : (g + 1) * dm.group, :].reshape(dm.keys, dm.width)
         for g in range(dm.groups)
     ]
-    code = jnp.concatenate([s.codes[layer, z] for z in range(dm.axes[0])], 1)
+    code = jnp.concatenate([s.codes[layer, z] for z in range(dm.axes[0])], 1)[0:1]
+    count = dm.first_unit
+    starts = [odd * dm.blocks for odd in range(dm.group_js)]
+    chosen = jnp.concatenate([one_hot((start, count), code, 0) for start in starts], 0)
+    attention = []
+    for g in range(dm.groups):
+        rows = dot_nn(chosen, shards[g]).astype(BF16)
+        attention += [rows[n * count : (n + 1) * count] for n in range(dm.group_js)]
+    order = row_order(dm, cols, dm.kind_blocks)
     for kind in range(4):
-        total = None
+        part = slice(kind * dm.kind_blocks, (kind + 1) * dm.kind_blocks)
+        rows = dot_nn(order, jnp.concatenate([rows[part] for rows in attention], 0)).astype(BF16)
+        if kind < 3:
+            s.w_qkv[layer, pl.ds(pl.multiple_of(kind * HEADS * HD + half * cols, 16), cols), :] = rows
+        else:
+            s.w_out[layer, pl.ds(pl.multiple_of(half * cols, 16), cols), :] = rows
+    yield
+    for odd, start in enumerate(starts):
+        chosen = one_hot((start + count, 2 * some), code, 0)
         for g in range(dm.groups):
-            part = dot_nn(one_hot((kind * cols, cols), code[g : g + 1, :], 0), shards[g])
-            total = part if total is None else total + part
-        total = total.astype(BF16)
-        if kind < 3:
-            s.w_qkv[layer, pl.ds(pl.multiple_of(kind * HEADS * HD + half * cols, 16), cols), :] = total
-        else:
-            s.w_out[layer, pl.ds(pl.multiple_of(half * cols, 16), cols), :] = total
-    yield
-    tile = min(256, dm.group_units)
+            rows = dot_nn(chosen, shards[g]).astype(BF16)
+            at = half * units + (g * dm.group_js + odd) * some
+            at = pl.ds(pl.multiple_of(at, 16), some)
+            s.w_up[layer, at, :] = rows[:some]
+            s.w_down[layer, at, :] = rows[some:]
+
+
+def put_grads(dm, s, kind, rows):
+    cols, size = dm.half_cols, dm.kind_blocks
+    order = row_order(dm, cols, size)
+    for half in range(dm.halves):
+        found = dot_tn(order, rows[half * cols : (half + 1) * cols]).astype(BF16)
+        for j in range(dm.block_rows):
+            s.grads[half, j // dm.group_js, j % dm.group_js, kind * size : (kind + 1) * size, :] = found[
+                j * size : (j + 1) * size
+            ]
+
+
+def permute_out(dm, layer, half, s):
     for g in range(dm.groups):
-        for target, first in ((s.w_up, 0), (s.w_down, dm.group_units)):
-            for start in range(0, dm.group_units, tile):
-                chosen = one_hot((first + start, tile), code[dm.groups : dm.groups + 1, :], 0)
-                at = pl.multiple_of(half * units + g * dm.group_units + start, 16)
-                target[layer, pl.ds(at, tile), :] = dot_nn(chosen, shards[g]).astype(BF16)
-
-
-def permute_out(dm, layer, half, s):
-    natural, units, size = dm.natural, dm.half_units, dm.group_units
-
-    def add(start, count):
-        rows = slice(start, start + count)
-        total = s.grads[half, rows, :].astype(F32) + s.grads_in[rows, :].astype(F32)
-        s.grads_in[rows, :] = total.astype(BF16)
-
-    for start in range(0, dm.half_rows, 256):
-        add(start, min(256, dm.half_rows - start))
-    per = dm.axes[1] * dm.axes[2] * dm.group
-
-    def piece(z):
-        codes = jnp.transpose(s.codes[layer, z])
+        for odd in range(dm.group_js):
+            total = s.grads[half, g, odd].astype(F32) + s.grads_in[g, odd].astype(F32)
+            s.grads_in[g, odd] = total.astype(BF16)
+
+    def pieces(places):
+        codes = [jnp.transpose(s.codes[layer, z])[:, 0:1] for z in places]
+        chosen = one_hot((0, dm.group_js * dm.blocks), jnp.concatenate(codes, 0), 1)
+        size = chosen.shape[0] // len(places)
         for g in range(dm.groups):
-            up, down = natural + g * size, natural + units + g * size
-            both = jnp.concatenate([s.grads_in[up : up + size, :], s.grads_in[down : down + size, :]], 0)
-            rows = dot_nn(one_hot((0, natural), codes[:, g : g + 1], 1), s.grads_in[:natural, :])
-            rows = rows + dot_nn(one_hot((0, 2 * size), codes[:, dm.groups : dm.groups + 1], 1), both)
-            s.gath[layer, z, :, :, g * dm.group : (g + 1) * dm.group, :] = rows.astype(BF16).reshape(
-                dm.axes[1], dm.axes[2], dm.group, dm.width
-            )
-
-    return piece
+            grads = s.grads_in[g].reshape(dm.group_js * dm.blocks, dm.width)
+            rows = dot_nn(chosen, grads).astype(BF16)
+            for n, z in enumerate(places):
+                s.gath[layer, z, :, :, g * dm.group : (g + 1) * dm.group, :] = rows[
+                    n * size : (n + 1) * size
+                ].reshape(dm.axes[1], dm.axes[2], dm.group, dm.width)
+
+    return pieces
 
 
 def prepare_codes(dm, slot_block, s):
@@ -148,7 +162,6 @@
     high = divide(block, 16)
     zero = jnp.zeros((16 - 2 * layers, blocks), F32)
     halves = jnp.concatenate([high, block - 16.0 * high, zero], 0).astype(BF16)
-    first = dm.natural // dm.block_rows
     per = dm.keys // dm.axes[0]
     size = per * max(1, 768 // per)
     for start in range(0, dm.keys, size):
@@ -167,27 +180,22 @@
         _, odd, padding = place((1, size))
         for layer in range(layers):
             block = 16.0 * parts[layer : layer + 1] + parts[layers + layer : layers + layer + 1]
-            rows = []
-            for g in range(dm.groups):
-                at = block * dm.block_rows + g * dm.group_js + odd
-                rows.append(jnp.where(padding | (block >= first), -1.0, at))
-            inner = block - first
-            at = odd * dm.unit_blocks + inner
-            at = jnp.where(inner < dm.unit_blocks, at, at - dm.unit_blocks + dm.group_units)
-            rows.append(jnp.where(padding | (inner < 0), -1.0, at))
-            rows.append(jnp.zeros((8 - len(rows), size), F32))
-            rows = jnp.concatenate(rows, 0)
+            row = jnp.where(padding, -1.0, odd * blocks + block)
+            rows = jnp.concatenate([row, jnp.zeros((7, size), F32)], 0)
             for z in range(start // per, (start + size) // per):
                 s.codes[layer, z] = rows[:, z * per - start : (z + 1) * per - start]
 
 
+def row_order(dm, rows, blocks):
+    here = lax.broadcasted_iota(jnp.int32, (rows, rows), 1)
+    inner = divide(here, blocks)
+    source = (here.astype(F32) - inner * blocks) * dm.block_rows + inner
+    same = source == lax.broadcasted_iota(jnp.int32, (rows, rows), 0).astype(F32)
+    return same.astype(F32).astype(BF16)
+
+
 def unit_order(dm):
-    units = dm.half_units
-    here = lax.broadcasted_iota(jnp.int32, (units, units), 1)
-    inner = divide(here, dm.unit_blocks)
-    source = (here.astype(F32) - inner * dm.unit_blocks) * dm.block_rows + inner
-    same = source == lax.broadcasted_iota(jnp.int32, (units, units), 0).astype(F32)
-    return same.astype(F32).astype(BF16)
+    return row_order(dm, dm.half_units, dm.unit_blocks)
 
 
 def reorder(dot, row, order):
@@ -412,19 +420,21 @@
 
 
 def backward_units(dm, layer, s):
-    tile, units = 256, dm.half_units
-    per_half = units // tile
+    tile, some = 2 * dm.unit_blocks, dm.unit_blocks
+    per_half = dm.half_units // tile
 
     def unit_tile(number):
         cols = pl.ds(pl.multiple_of(number * tile, tile), tile)
         grad = dot_nt(s.low_g[...], s.w_down[layer, cols, :])
         grad = (grad * s.slope[layer, :, cols].astype(F32)).astype(BF16)
         s.slope[layer, :, cols] = grad
-        half, at = number // per_half, pl.multiple_of((number % per_half) * tile, tile)
-        s.grads[half, pl.ds(dm.natural + units + at, tile), :] = dot_tn(
-            s.act[layer, :, cols], s.low_g[...]
-        ).astype(BF16)
-        s.grads[half, pl.ds(dm.natural + at, tile), :] = dot_tn(grad, s.low_b[layer]).astype(BF16)
+        half, first = number // per_half, (number % per_half) * 2
+        down = dot_tn(s.act[layer, :, cols], s.low_g[...]).astype(BF16)
+        up = dot_tn(grad, s.low_b[layer]).astype(BF16)
+        for n in range(2):
+            g, odd = (first + n) // dm.group_js, (first + n) % dm.group_js
+            for value, start in ((up, dm.first_unit), (down, dm.first_unit + some)):
+                s.grads[half, g, odd, start : start + some, :] = value[n * some : (n + 1) * some]
 
     loop(FF // tile, unit_tile)
 
@@ -451,10 +461,7 @@
 
 
 def backward_out(dm, layer, s):
-    cols = dm.half_cols
-    value = dot_tn(s.att[layer], s.low_g[...]).astype(BF16)
-    for half in range(dm.halves):
-        s.grads[half, 3 * cols : dm.natural, :] = value[half * cols : (half + 1) * cols]
+    put_grads(dm, s, 3, dot_tn(s.att[layer], s.low_g[...]).astype(BF16))
 
     def out_project(image):
         rows = image_rows(dm, image)
@@ -492,11 +499,10 @@
 
 
 def backward_rows(dm, layer, s):
-    wide, cols = HEADS * HD, dm.half_cols
+    wide = HEADS * HD
     for kind in range(3):
-        value = dot_tn(s.qkv[layer, :, kind * wide : (kind + 1) * wide], s.low_a[layer]).astype(BF16)
-        for half in range(dm.halves):
-            s.grads[half, kind * cols : (kind + 1) * cols, :] = value[half * cols : (half + 1) * cols]
+        value = dot_tn(s.qkv[layer, :, kind * wide : (kind + 1) * wide], s.low_a[layer])
+        put_grads(dm, s, kind, value.astype(BF16))
 
 
 def backward_sums(dm, layer, s):
@@ -595,7 +601,8 @@
     depth, rows, cols = dm.axes
     cross = depth * (cols + rows - 2)
     vectors = 1 + (depth - 1) + (rows * cols - 1)
-    return dm.layers * (depth - 1 + 2 * cross + 6 + 2 + vectors + 1 + 2 * dm.images)
+    ends = depth - 1 + rows * cols - 1
+    return dm.layers * (depth - 1 + 2 * cross + ends + 6 + 2 + vectors + 1 + 2 * dm.images)
 
 
 def start_all(copies):
@@ -608,77 +615,15 @@
         copy.wait()
 
 
-class Gather:
-    def __init__(self, dm, net, s, layer):
-        self.dm, self.net, self.layer, self.buf = dm, net, layer, s.gath.at[layer]
-        self.head = pl.ds(0, dm.first_rows)
-        self.tail = pl.ds(dm.first_rows, dm.shard_rows - dm.first_rows)
-        depth = dm.axes[0]
-        self.order = sorted(range(1, depth), key=lambda o: min(o, depth - o))
-
-    def keys(self, name, piece, number):
-        _, rows, cols = self.dm.axes
-        count = rows + cols - 2
-        return (name, self.dm.axes[0] * count, piece * count + number)
-
-    def one(self, offset):
-        ref = self.buf.at[self.net.place]
-        key = ("one", self.dm.axes[0] - 1, offset - 1)
-        return [self.net.copy(key, self.layer, ref, ref, self.net.on_axis(0, offset))]
-
-    def pairs(self, name, piece, pairs):
-        copies = []
-        for ref, axis in pairs:
-            for o in range(1, self.dm.axes[axis]):
-                key = self.keys(name, piece, len(copies))
-                copies.append(self.net.copy(key, self.layer, ref, ref, self.net.on_axis(axis, o)))
-        return copies
-
-    def two(self, piece):
-        at, (_, y, x) = self.net.along(0, -piece), self.net.place
-        return self.pairs(
-            "two", piece, [(self.buf.at[at, y, x, self.head], 2), (self.buf.at[at, y, x, self.tail], 1)]
-        )
-
-    def three(self, piece):
-        at, (_, y, x) = self.net.along(0, -piece), self.net.place
-        return self.pairs(
-            "three", piece, [(self.buf.at[at, y, :, self.head], 1), (self.buf.at[at, :, x, self.tail], 2)]
-        )
-
-    def begin(self):
-        for offset in range(1, self.dm.axes[0]):
-            start_all(self.one(offset))
-        start_all(self.two(0))
-
-    def steps(self):
-        found = []
-        before = 0
-        for piece in self.order + [None]:
-
-            def step(before=before, piece=piece):
-                if piece is not None:
-                    wait_all(self.one(piece))
-                    start_all(self.two(piece))
-                wait_all(self.two(before))
-                start_all(self.three(before))
-
-            found.append(step)
-            before = piece
-        return found
-
-    def end(self):
-        for piece in range(self.dm.axes[0]):
-            wait_all(self.three(piece))
-
-
-class Scatter:
+class Parts:
     def __init__(self, dm, net, s, layer):
         self.dm, self.net, self.s, self.layer, self.buf = dm, net, s, layer, s.gath.at[layer]
+        self.most = pl.ds(0, dm.most_rows)
         self.head = pl.ds(0, dm.first_rows)
-        self.tail = pl.ds(dm.first_rows, dm.shard_rows - dm.first_rows)
-
-    def pairs(self, name, piece, parts):
+        self.tail = pl.ds(dm.first_rows, dm.most_rows - dm.first_rows)
+        self.last = pl.ds(dm.most_rows, dm.last_rows)
+
+    def pairs(self, name, layer, piece, parts):
         copies = []
         _, rows, cols = self.dm.axes
         count = rows + cols - 2
@@ -686,13 +631,102 @@
             for o in range(1, self.dm.axes[axis]):
                 key = (name, self.dm.axes[0] * count, piece * count + len(copies))
                 source, target = make(self.net.along(axis, o), o - 1)
-                copies.append(self.net.copy(key, 0, source, target, self.net.on_axis(axis, o)))
+                copies.append(
+                    self.net.copy(key, layer, source, target, self.net.on_axis(axis, o))
+                )
         return copies
 
+    def plane(self, layer, make):
+        offsets = self.net.plane()
+        copies = []
+        for n, (p, q) in enumerate(offsets):
+            source, target = make(self.net.along(1, p), self.net.along(2, q), n)
+            copies.append(
+                self.net.copy(
+                    ("ends", len(offsets), n), layer, source, target, self.net.device(0, p, q)
+                )
+            )
+        return copies
+
+
+class Gather(Parts):
+    def __init__(self, dm, net, s, layer):
+        super().__init__(dm, net, s, layer)
+        depth = dm.axes[0]
+        self.order = sorted(range(1, depth), key=lambda o: min(o, depth - o))
+
+    def one(self, offset):
+        ref = self.buf.at[(*self.net.place, self.most)]
+        key = ("one", self.dm.axes[0] - 1, offset - 1)
+        return [self.net.copy(key, self.layer, ref, ref, self.net.on_axis(0, offset))]
+
+    def two(self, piece):
+        at, (_, y, x) = self.net.along(0, -piece), self.net.place
+        a, b = self.buf.at[at, y, x, self.head], self.buf.at[at, y, x, self.tail]
+        return self.pairs(
+            "two", self.layer, piece, [(2, lambda to, n: (a, a)), (1, lambda to, n: (b, b))]
+        )
+
+    def three(self, piece):
+        at, (_, y, x) = self.net.along(0, -piece), self.net.place
+        a, b = self.buf.at[at, y, :, self.head], self.buf.at[at, :, x, self.tail]
+        return self.pairs(
+            "three", self.layer, piece, [(1, lambda to, n: (a, a)), (2, lambda to, n: (b, b))]
+        )
+
+    def near(self):
+        if not self.dm.last_rows:
+            return []
+        ref = self.buf.at[(*self.net.place, self.last)]
+        return self.plane(self.layer, lambda y, x, n: (ref, ref))
+
+    def far(self):
+        if not self.dm.last_rows:
+            return []
+        ref = self.buf.at[self.net.place[0], :, :, self.last]
+        size = self.dm.axes[0]
+        return [
+            self.net.copy(("far", size - 1, o - 1), self.layer, ref, ref, self.net.on_axis(0, o))
+            for o in range(1, size)
+        ]
+
+    def begin(self):
+        for offset in range(1, self.dm.axes[0]):
+            start_all(self.one(offset))
+        start_all(self.two(0))
+        start_all(self.near())
+
+    def steps(self):
+        found = []
+        before = 0
+        for number, piece in enumerate(self.order + [None]):
+
+            def step(before=before, piece=piece, number=number):
+                if piece is not None:
+                    wait_all(self.one(piece))
+                    start_all(self.two(piece))
+                wait_all(self.two(before))
+                start_all(self.three(before))
+                if number == 0:
+                    wait_all(self.near())
+                    start_all(self.far())
+
+            found.append(step)
+            before = piece
+        return found
+
+    def end(self):
+        for piece in range(self.dm.axes[0]):
+            wait_all(self.three(piece))
+        wait_all(self.far())
+
+
+class Scatter(Parts):
     def one(self, piece):
         at, s, buf = self.net.along(0, piece), self.s, self.buf
         return self.pairs(
             "three",
+            0,
             piece,
             [
                 (1, lambda to, n: (buf.at[at, to, :, self.head], s.one_a.at[piece, n])),
@@ -704,6 +738,7 @@
         at, s, buf, (_, y, x) = self.net.along(0, piece), self.s, self.buf, self.net.place
         return self.pairs(
             "two",
+            0,
             piece,
             [
                 (2, lambda to, n: (buf.at[at, y, to, self.head], s.two_a.at[piece, n])),
@@ -713,17 +748,35 @@
 
     def three(self, piece):
         _, y, x = self.net.place
-        source = self.buf.at[self.net.along(0, piece), y, x]
+        source = self.buf.at[self.net.along(0, piece), y, x, self.most]
         target = self.s.three.at[self.layer, piece - 1]
         key = ("one", self.dm.axes[0] - 1, piece - 1)
         turn = self.dm.layers - 1 - self.layer
         return self.net.copy(key, turn, source, target, self.net.device(piece, 0, 0))
+
+    def far(self, piece):
+        source = self.buf.at[self.net.along(0, piece), :, :, self.last]
+        key = ("far", self.dm.axes[0] - 1, piece - 1)
+        return self.net.copy(key, 0, source, self.s.far.at[piece - 1], self.net.device(piece, 0, 0))
+
+    def near(self):
+        z = self.net.place[0]
+        return self.plane(0, lambda y, x, n: (self.buf.at[z, y, x, self.last], self.s.near.at[n]))
 
     def add(self, at, parts):
         value = self.buf[at].astype(F32)
         for part in parts:
             value = value + part.astype(F32)
         self.buf[at] = value.astype(BF16)
+
+    def begin(self, piece):
+        if self.dm.last_rows:
+
+            @pl.when(piece > 0)
+            def _():
+                self.far(piece).start()
+
+        start_all(self.one(piece))
 
     def second(self, piece):
         _, rows, cols = self.dm.axes
@@ -744,12 +797,29 @@
         def _():
             self.three(piece).start()
 
+    def second_last(self):
+        if self.dm.last_rows:
+            pieces = range(1, self.dm.axes[0])
+            wait_all([self.far(piece) for piece in pieces])
+            z = self.net.place[0]
+            at = (z, slice(None), slice(None), self.last)
+            self.add(at, [self.s.far[piece - 1] for piece in pieces])
+            start_all(self.near())
+
+    def third_last(self):
+        if self.dm.last_rows:
+            copies = self.near()
+            wait_all(copies)
+            self.add((*self.net.place, self.last), [self.s.near[n] for n in range(len(copies))])
+
     def end(self):
-        value = self.buf[self.net.place].astype(F32)
+        value = self.buf[(*self.net.place, self.most)].astype(F32)
         for piece in range(1, self.dm.axes[0]):
             self.three(piece).wait()
             value = value + self.s.three[self.layer, piece - 1].astype(F32)
-        return value
+        self.s.rows[self.most, :] = value
+        if self.dm.last_rows:
+            self.s.rows[self.last, :] = self.buf[(*self.net.place, self.last)].astype(F32)
 
 
 class Totals:
@@ -814,7 +884,7 @@
 def scratch_shapes(dm):
     layers, tokens, width, wide = dm.layers, dm.tokens, dm.width, HEADS * HD
     depth, rows, cols = dm.axes
-    head, tail = dm.first_rows, dm.shard_rows - dm.first_rows
+    head, tail = dm.first_rows, dm.most_rows - dm.first_rows
     vmem, copies = pltpu.VMEM, copies_needed(dm)
     return dict(
         hid=vmem((tokens, width), F32),
@@ -835,14 +905,16 @@
         w_out=vmem((layers, wide, width), BF16),
         w_up=vmem((layers, FF, width), BF16),
         w_down=vmem((layers, FF, width), BF16),
-        grads=vmem((dm.halves, dm.half_rows, width), BF16),
-        grads_in=vmem((dm.half_rows, width), BF16),
+        grads=vmem((dm.halves, dm.groups, dm.group_js, dm.blocks, width), BF16),
+        grads_in=vmem((dm.groups, dm.group_js, dm.blocks, width), BF16),
         gath=vmem((layers, depth, rows, cols, dm.shard_rows, width), BF16),
         one_a=vmem((depth, rows - 1, cols, head, width), BF16),
         one_b=vmem((depth, cols - 1, rows, tail, width), BF16),
         two_a=vmem((depth, cols - 1, head, width), BF16),
         two_b=vmem((depth, rows - 1, tail, width), BF16),
-        three=vmem((layers, depth - 1, dm.shard_rows, width), BF16),
+        three=vmem((layers, depth - 1, dm.most_rows, width), BF16),
+        far=vmem((depth - 1, rows, cols, max(16, dm.last_rows), width), BF16),
+        near=vmem((rows * cols - 1, max(16, dm.last_rows), width), BF16),
         rows=vmem((dm.shard_rows, width), F32),
         tok_in=vmem((dm.images, dm.seq, width), F32),
         tok_out=vmem((dm.images, dm.seq, width), F32),
@@ -1000,7 +1072,7 @@
     load_tokens(dm, s.tok_in, s.hid, s.columns)
 
     def put_rows(layer):
-        s.rows[...] = Scatter(dm, net, s, layer).end()
+        Scatter(dm, net, s, layer).end()
         for j in range(dm.block_rows):
             matrix[0, layer, j] = s.rows[j * dm.slots : (j + 1) * dm.slots, :]
 
@@ -1010,9 +1082,10 @@
             vec_out[0, r, layer : layer + 1, :] = value[r : r + 1]
 
     def share(layer, number):
-        rows = (pl.ds(dm.natural, 2 * units), pl.ds(0, dm.natural))[number]
-        source = s.grads.at[1 - net.core, rows]
-        return net.copy(("shares", 2, number), layer, source, s.grads_in.at[rows], net.sibling())
+        start = dm.first_unit
+        rows = (pl.ds(start, dm.blocks - start), pl.ds(0, start))[number]
+        source, target = s.grads.at[1 - net.core, :, :, rows], s.grads_in.at[:, :, rows]
+        return net.copy(("shares", 2, number), layer, source, target, net.sibling())
 
     def backward(turn):
         layer = dm.layers - 1 - turn
@@ -1031,36 +1104,35 @@
             if name == "units":
                 when_later(pl.semaphore_wait, s.core_credit, 1)
                 share(layer, 0).start()
-            if name in ("units", "down", "mid", "out"):
-                count = -(-depth // 4)
+            if name in ("units", "mid", "attend"):
+                count = depth // 2 if name == "units" else depth // 4
                 now, order = order[:count], order[count:]
                 for piece in now:
                     when_later(before.second, piece)
-            if name == "out":
-                order = list(range(depth - 1, -1, -1))
-            if name in ("attend", "attended"):
-                count = depth // 2
-                now, order = order[:count], order[count:]
-                for piece in now:
+            if name == "down":
+                when_later(before.second_last)
+            if name == "attended":
+                when_later(before.third_last)
+                for piece in range(depth - 1, -1, -1):
                     when_later(before.third, piece)
-            if name == "attended":
                 when_later(net.greet, s.credit)
                 when_later(totals_before.third)
             if name == "rows":
                 share(layer, 1).start()
-            if name == "more":
+            if name == "project":
                 wait_all([share(layer, 0), share(layer, 1)])
                 fill = permute_out(dm, layer, net.core, s)
                 when_later(net.met, s.credit)
                 scatter = Scatter(dm, net, s, layer)
 
-                def piece_out(number, carry):
-                    piece = depth - 1 - number
-                    fill(net.along(0, piece))
-                    start_all(scatter.one(piece))
+                def pieces_out(number, carry):
+                    pieces = [depth - 1 - 2 * number, depth - 2 - 2 * number]
+                    fill([net.along(0, piece) for piece in pieces])
+                    for piece in pieces:
+                        scatter.begin(piece)
                     return carry
 
-                lax.fori_loop(0, depth, piece_out, 0)
+                lax.fori_loop(0, depth // 2, pieces_out, 0)
 
                 @pl.when(layer > 0)
                 def _():
@@ -1078,10 +1150,12 @@
     scatter, totals = Scatter(dm, net, s, 0), Totals(dm, net, s, 0, first)
     totals.second()
     loop(depth, lambda n: scatter.second(depth - 1 - n))
+    scatter.second_last()
     put_vectors(1)
     put_rows(1)
     totals.third()
     loop(depth, lambda n: scatter.third(depth - 1 - n))
+    scatter.third_last()
     put_vectors(0)
     put_rows(0)
     wait_all(tokens.store(grad_in, 1))

time: 142 us -> 134 us (0.944)
  Pallas kernels: 141 us -> 133 us
    pallas_call x1, Pallas kernels: 135 us -> 127 us  [run_step(): pl.pallas_call(functools.partial(step_kernel, dm, tuple(shapes)), out_sha...]
where the time goes in v1:
time: 134 us
  Pallas kernels  133 us (99%)
    pallas_call x1, Pallas kernels, run_step(): pl.pallas_call(functools.partial(step_kernel, dm, tuple(shapes)), out_sha...  127 us
    pallas_call x1, Pallas kernels, run_finish(): pl.pallas_call(functools.partial(finish_kernel, parts), out_shape=tuple((...  5.52 us

profile of v1, /device:TPU:0, one launch (start us, length us, event | category | flops | bytes accessed | tf_op | source)
XLA Modules:
  0.0 133.7 jit_solution(16491994292227652379)
XLA Ops:
  0.6 127.4 %shard_map.161 = (f32[198,8,384]{2,1,0:T(8,128)}, f32[198,8,384]{2,1,0:T(8,128)}, f32[1,2,6,24,384]{4,3,2,1,0:T(8,128)}, f32[1,6,2,384]{3,2,1,0:T(2,128)}) custom-call(f32[198,8,384]{2,1,0:T(8,128)} %bitcast.16, s32[8,198]{1,0:T(8,128)} %keep_mask.1, f32[198,8,384]{2,1,0:T(8,128)} %bitcast.17, s32[2,384]{1,0:T(2,128)} %slot_block.1, ...), custom_call_target="tpu_custom_call" | custom-call | tf_op jit(solution)/shard_map/pallas_call | solution.py:1173
  128.0 5.5 %shard_map.162 = (f32[198,8,384]{2,1,0:T(8,128)}, f32[198,8,384]{2,1,0:T(8,128)}, f32[1,2,6,24,384]{4,3,2,1,0:T(8,128)}, f32[1,2,6,24,384]{4,3,2,1,0:T(8,128)}, ...) custom-call(f32[198,8,384]{2,1,0:T(8,128)} %get-tuple-element.20.ref, ...), custom_call_target="tpu_custom_call" | custom-call | tf_op jit(solution)/shard_map/pallas_call | solution.py:1245

commit v2 on v1

--- a/solution.py
+++ b/solution.py
@@ -20,6 +20,7 @@
 DECAY_MATRIX = 0.05
 EPS_ADAM = 1e-08
 NEG_FILL = -1e30
+LOG2_E = 1.4426950408889634
 
 F32 = jnp.float32
 MESH = pl.DeviceIdType.MESH
@@ -332,8 +333,8 @@
             out = None
             for side, lanes in enumerate(halves):
                 scores = dot_nt(k * lanes, q)
-                scores = jnp.where(keep > 0, scores * HD ** (-0.5), NEG_FILL)
-                exponent = jnp.exp(scores - jnp.max(scores, 0, keepdims=True))
+                scores = jnp.where(keep > 0, scores * (HD ** (-0.5) * LOG2_E), NEG_FILL)
+                exponent = jnp.exp2(scores - jnp.max(scores, 0, keepdims=True))
                 probs = (exponent * (1.0 / jnp.sum(exponent, 0, keepdims=True))).astype(BF16)
                 s.probs[layer, image * HEADS + 2 * pair + side] = probs
                 part = dot_tn(probs, v * lanes)
@@ -650,11 +651,6 @@
 
 
 class Gather(Parts):
-    def __init__(self, dm, net, s, layer):
-        super().__init__(dm, net, s, layer)
-        depth = dm.axes[0]
-        self.order = sorted(range(1, depth), key=lambda o: min(o, depth - o))
-
     def one(self, offset):
         ref = self.buf.at[(*self.net.place, self.most)]
         key = ("one", self.dm.axes[0] - 1, offset - 1)
@@ -690,30 +686,25 @@
             for o in range(1, size)
         ]
 
-    def begin(self):
+    def along_depth(self):
         for offset in range(1, self.dm.axes[0]):
             start_all(self.one(offset))
+
+    def begin(self):
         start_all(self.two(0))
         start_all(self.near())
 
-    def steps(self):
-        found = []
-        before = 0
-        for number, piece in enumerate(self.order + [None]):
-
-            def step(before=before, piece=piece, number=number):
-                if piece is not None:
-                    wait_all(self.one(piece))
-                    start_all(self.two(piece))
-                wait_all(self.two(before))
-                start_all(self.three(before))
-                if number == 0:
-                    wait_all(self.near())
-                    start_all(self.far())
-
-            found.append(step)
-            before = piece
-        return found
+    def cross(self, piece):
+        wait_all(self.one(piece))
+        start_all(self.two(piece))
+
+    def spread(self, piece):
+        wait_all(self.two(piece))
+        start_all(self.three(piece))
+
+    def spread_last(self):
+        wait_all(self.near())
+        start_all(self.far())
 
     def end(self):
         for piece in range(self.dm.axes[0]):
@@ -1008,6 +999,7 @@
     start_all(tokens.load(hidden))
     own_shard(dm, master, net, s)
     net.met(barrier)
+    gathers[0].along_depth()
     gathers[0].begin()
     pack_vectors(dm, vectors, first, s)
     other_vec = net.copy(("vectors", 1, 0), 0, s.vec_own, s.vec_in, net.sibling())
@@ -1019,10 +1011,15 @@
     start_all(tokens.load(cotangent))
     other_vec.wait()
     s.vec[...] = s.vec_own[...] + s.vec_in[...]
-    for step in gathers[0].steps():
-        step()
+    gathers[0].spread(0)
+    gathers[0].spread_last()
+    for piece in range(1, depth):
+        gathers[0].cross(piece)
+        if piece > 1:
+            gathers[0].spread(piece - 1)
+    gathers[1].along_depth()
+    gathers[0].spread(depth - 1)
     gathers[1].begin()
-    steps = gathers[1].steps()
 
     def weights(layer):
         parts = [(s.w_qkv, kind * HEADS * HD + net.core * cols, cols) for kind in range(3)]
@@ -1040,12 +1037,31 @@
         for name, phase in FORWARD:
             phase(dm, layer, s)
             if name == "norm":
+
+                more = layer + 1 < dm.layers
+                pl.when(more)(lambda: gathers[1].cross(1))
                 Gather(dm, net, s, layer).end()
+
+                @pl.when(more)
+                def _():
+                    gathers[1].spread(0)
+                    gathers[1].spread_last()
+                    for piece in range(2, depth // 2 + 1):
+                        gathers[1].cross(piece)
+
                 parts = permute_in(dm, layer, net.core, s)
                 next(parts)
                 start_all(shares[:4])
                 next(parts, None)
                 start_all(shares[4:])
+
+                @pl.when(more)
+                def _():
+                    for piece in range(depth // 2 + 1, depth):
+                        gathers[1].cross(piece)
+                    for piece in range(1, depth // 2):
+                        gathers[1].spread(piece)
+
                 wait_all(shares[:3])
             if name == "attend":
                 shares[3].wait()
@@ -1053,15 +1069,14 @@
                 shares[4].wait()
             if name == "up":
                 shares[5].wait()
-            if name in ("norm", "project", "attend", "mid"):
-                now = [steps.pop(0)]
-                if name == "mid":
-                    now, steps[:] = now + steps, []
+            if name in ("project", "attend"):
+                some = depth // 4
+                pieces = range(depth // 2, depth - some) if name == "project" else range(depth - some, depth)
 
                 @pl.when(layer + 1 < dm.layers)
-                def _(now=now):
-                    for step in now:
-                        step()
+                def _(pieces=pieces):
+                    for piece in pieces:
+                        gathers[1].spread(piece)
 
     lax.fori_loop(0, dm.layers, lambda i, c: (forward(i), c)[1], 0)
     for image in range(dm.images):
@@ -1100,7 +1115,8 @@
         for name, phase in BACKWARD:
             phase(dm, layer, s)
             if name == "start":
-                when_later(totals_before.second)
+                for piece in range(depth // 2 - 1, -1, -1):
+                    when_later(before.begin, piece)
             if name == "units":
                 when_later(pl.semaphore_wait, s.core_credit, 1)
                 share(layer, 0).start()
@@ -1109,6 +1125,8 @@
                 now, order = order[:count], order[count:]
                 for piece in now:
                     when_later(before.second, piece)
+            if name == "units":
+                when_later(totals_before.second)
             if name == "down":
                 when_later(before.second_last)
             if name == "attended":
@@ -1125,14 +1143,11 @@
                 when_later(net.met, s.credit)
                 scatter = Scatter(dm, net, s, layer)
 
-                def pieces_out(number, carry):
+                for number in range(depth // 2):
                     pieces = [depth - 1 - 2 * number, depth - 2 - 2 * number]
                     fill([net.along(0, piece) for piece in pieces])
-                    for piece in pieces:
+                    for piece in pieces if number < depth // 4 else []:
                         scatter.begin(piece)
-                    return carry
-
-                lax.fori_loop(0, depth // 2, pieces_out, 0)
 
                 @pl.when(layer > 0)
                 def _():
@@ -1148,14 +1163,22 @@
         s.tok_out[image] = s.hid[rows, :]
     start_all(tokens.store(grad_in, 1))
     scatter, totals = Scatter(dm, net, s, 0), Totals(dm, net, s, 0, first)
-    totals.second()
-    loop(depth, lambda n: scatter.second(depth - 1 - n))
+    events = [(totals.second,)]
+    for piece in range(depth - 1, -1, -1):
+        events.append((scatter.second, piece))
+        if piece == depth // 2:
+            events.append((totals.third,))
+        if piece >= depth // 2:
+            events.append((scatter.begin, piece - depth // 2))
+        if piece < depth - 1:
+            events.append((scatter.third, piece + 1))
+    for event, *args in events:
+        event(*args)
     scatter.second_last()
+    scatter.third(0)
+    scatter.third_last()
     put_vectors(1)
     put_rows(1)
-    totals.third()
-    loop(depth, lambda n: scatter.third(depth - 1 - n))
-    scatter.third_last()
     put_vectors(0)
     put_rows(0)
     wait_all(tokens.store(grad_in, 1))

time: 134 us -> 127 us (0.948)
  Pallas kernels: 133 us -> 126 us
    pallas_call x1, Pallas kernels: 127 us -> 121 us  [run_step(): pl.pallas_call(functools.partial(step_kernel, dm, tuple(shapes)), out_sha...]
where the time goes in v2:
time: 127 us
  Pallas kernels  126 us (99%)
    pallas_call x1, Pallas kernels, run_step(): pl.pallas_call(functools.partial(step_kernel, dm, tuple(shapes)), out_sha...  121 us
    pallas_call x1, Pallas kernels, run_finish(): pl.pallas_call(functools.partial(finish_kernel, parts), out_shape=tuple((...  5.52 us

profile of v2, /device:TPU:0, one launch (start us, length us, event | category | flops | bytes accessed | tf_op | source)
XLA Modules:
  0.0 127.2 jit_solution(7448890093205992101)
XLA Ops:
  0.6 120.9 %shard_map.161 = (f32[198,8,384]{2,1,0:T(8,128)}, f32[198,8,384]{2,1,0:T(8,128)}, f32[1,2,6,24,384]{4,3,2,1,0:T(8,128)}, f32[1,6,2,384]{3,2,1,0:T(2,128)}) custom-call(f32[198,8,384]{2,1,0:T(8,128)} %bitcast.16, s32[8,198]{1,0:T(8,128)} %keep_mask.1, f32[198,8,384]{2,1,0:T(8,128)} %bitcast.17, s32[2,384]{1,0:T(2,128)} %slot_block.1, ...), custom_call_target="tpu_custom_call" | custom-call | tf_op jit(solution)/shard_map/pallas_call | solution.py:1196
  121.5 5.5 %shard_map.162 = (f32[198,8,384]{2,1,0:T(8,128)}, f32[198,8,384]{2,1,0:T(8,128)}, f32[1,2,6,24,384]{4,3,2,1,0:T(8,128)}, f32[1,2,6,24,384]{4,3,2,1,0:T(8,128)}, ...) custom-call(f32[198,8,384]{2,1,0:T(8,128)} %get-tuple-element.20.ref, ...), custom_call_target="tpu_custom_call" | custom-call | tf_op jit(solution)/shard_map/pallas_call | solution.py:1268

commit v3 on v2

--- a/solution.py
+++ b/solution.py
@@ -872,7 +872,7 @@
     pass
 
 
-def scratch_shapes(dm):
+def scratch_shapes(dm, operands=None):
     layers, tokens, width, wide = dm.layers, dm.tokens, dm.width, HEADS * HD
     depth, rows, cols = dm.axes
     head, tail = dm.first_rows, dm.most_rows - dm.first_rows
@@ -922,6 +922,8 @@
         send_sems=pltpu.SemaphoreType.DMA((copies,)),
         recv_sems=pltpu.SemaphoreType.DMA((copies,)),
         load_sems=pltpu.SemaphoreType.DMA((dm.images,)),
+        input_sems=pltpu.SemaphoreType.DMA((4,)),
+        **{name: vmem(array.shape, array.dtype) for name, array in (operands or {}).items()},
         store_sems=pltpu.SemaphoreType.DMA((dm.images,)),
         credit=pltpu.SemaphoreType.REGULAR,
         core_credit=pltpu.SemaphoreType.REGULAR,
@@ -984,10 +986,17 @@
         s.gath[layer, z, y, x] = s.rows[...].astype(BF16)
 
 
-def step_kernel(dm, names, hidden, keep_mask, cotangent, slot_block, master, vectors, acts, grad_in, matrix, vec_out, *scratch):
+def step_kernel(dm, names, hidden, keep_far, cotangent, slots_far, master_far, vectors_far, acts, grad_in, matrix, vec_out, *scratch):
     s = Refs()
     for name, ref in zip(names, scratch):
         setattr(s, name, ref)
+    master, vectors, slot_block, keep_mask = s.master, s.vectors, s.slot_block, s.keep_mask
+    inputs = [
+        pltpu.make_async_copy(far, here, s.input_sems.at[n])
+        for n, (far, here) in enumerate(
+            ((master_far, master), (vectors_far, vectors), (slots_far, slot_block), (keep_far, keep_mask))
+        )
+    ]
     net = Net(dm, s)
     first = net.core == 0
     tokens = Tokens(dm, net, s)
@@ -996,11 +1005,14 @@
     gathers = [Gather(dm, net, s, layer) for layer in range(dm.layers)]
     barrier = pltpu.get_barrier_semaphore()
     net.greet(barrier)
+    start_all(inputs)
     start_all(tokens.load(hidden))
+    inputs[0].wait()
     own_shard(dm, master, net, s)
     net.met(barrier)
     gathers[0].along_depth()
     gathers[0].begin()
+    wait_all(inputs[1:])
     pack_vectors(dm, vectors, first, s)
     other_vec = net.copy(("vectors", 1, 0), 0, s.vec_own, s.vec_in, net.sibling())
     other_vec.start()
@@ -1120,9 +1132,8 @@
             if name == "units":
                 when_later(pl.semaphore_wait, s.core_credit, 1)
                 share(layer, 0).start()
-            if name in ("units", "mid", "attend"):
-                count = depth // 2 if name == "units" else depth // 4
-                now, order = order[:count], order[count:]
+            if name in ("units", "down", "out", "attend"):
+                now, order = order[: depth // 4], order[depth // 4 :]
                 for piece in now:
                     when_later(before.second, piece)
             if name == "units":
@@ -1137,7 +1148,8 @@
                 when_later(totals_before.third)
             if name == "rows":
                 share(layer, 1).start()
-            if name == "project":
+            if name == "end":
+                Totals(dm, net, s, layer, first).begin()
                 wait_all([share(layer, 0), share(layer, 1)])
                 fill = permute_out(dm, layer, net.core, s)
                 when_later(net.met, s.credit)
@@ -1154,8 +1166,6 @@
                     pl.semaphore_signal(
                         s.core_credit, inc=1, device_id=net.sibling(), device_id_type=MESH
                     )
-        Totals(dm, net, s, layer, first).begin()
-
     lax.fori_loop(0, dm.layers, lambda i, c: (backward(i), c)[1], 0)
     wait_all(tokens.store(acts, 0))
     for image in range(dm.images):
@@ -1185,7 +1195,10 @@
 
 
 def run_step(dm, hidden_in, keep_mask, cotangent, slot_block, master, vector_master):
-    shapes = scratch_shapes(dm)
+    operands = dict(
+        master=master, vectors=vector_master, slot_block=slot_block, keep_mask=keep_mask
+    )
+    shapes = scratch_shapes(dm, operands)
     out_shape = (
         jax.ShapeDtypeStruct(hidden_in.shape, F32),
         jax.ShapeDtypeStruct(hidden_in.shape, F32),
@@ -1196,7 +1209,7 @@
     return pl.pallas_call(
         functools.partial(step_kernel, dm, tuple(shapes)),
         out_shape=out_shape,
-        in_specs=[far, full, far, full, full, full],
+        in_specs=[far] * 6,
         out_specs=[far, far, full, full],
         scratch_shapes=list(shapes.values()),
         compiler_params=pltpu.CompilerParams(
@@ -1243,8 +1256,11 @@
         pltpu.make_async_copy(vector_done.at[n], ref, store_sems.at[3 + n])
         for n, ref in enumerate(vector_out)
     ]
-    start_all(vector_loads + matrix_loads + loads)
-    wait_all(vector_loads + matrix_loads)
+    start_all(loads + matrix_loads + vector_loads)
+    for load, store in zip(loads, stores):
+        load.wait()
+        store.start()
+    wait_all(matrix_loads + vector_loads)
 
     def adam(held, done, at, rate, decay):
         grad, weight, one, two = (held[(n, *at)] for n in range(4))
@@ -1255,9 +1271,6 @@
         adam(matrix_in, matrix_done, (0, layer), RATE_MATRIX, DECAY_MATRIX)
     adam(vector_in, vector_done, (0,), RATE_VECTOR, 0.0)
     start_all(results)
-    for load, store in zip(loads, stores):
-        load.wait()
-        store.start()
     wait_all(stores + results)
 
 

time: 127 us -> 126 us (level)
  no operation moved by 1% of the time
where the time goes in v3:
time: 126 us
  Pallas kernels  125 us (99%)
    pallas_call x1, Pallas kernels, run_step(): pl.pallas_call(functools.partial(step_kernel, dm, tuple(shapes)), out_sha...  120 us
    pallas_call x1, Pallas kernels, run_finish(): pl.pallas_call(functools.partial(finish_kernel, parts), out_shape=tuple((...  5.05 us

profile of v3, /device:TPU:0, one launch (start us, length us, event | category | flops | bytes accessed | tf_op | source)
XLA Modules:
  0.0 125.5 jit_solution(14094614180720137685)
XLA Ops:
  0.6 119.7 %shard_map.161 = (f32[198,8,384]{2,1,0:T(8,128)}, f32[198,8,384]{2,1,0:T(8,128)}, f32[1,2,6,24,384]{4,3,2,1,0:T(8,128)}, f32[1,6,2,384]{3,2,1,0:T(2,128)}) custom-call(f32[198,8,384]{2,1,0:T(8,128)} %bitcast.16, s32[8,198]{1,0:T(8,128)} %keep_far.1, f32[198,8,384]{2,1,0:T(8,128)} %bitcast.17, s32[2,384]{1,0:T(2,128)} %slots_far.1, ...), custom_call_target="tpu_custom_call" | custom-call | tf_op jit(solution)/shard_map/pallas_call | solution.py:1209
  120.3 5.1 %shard_map.162 = (f32[198,8,384]{2,1,0:T(8,128)}, f32[198,8,384]{2,1,0:T(8,128)}, f32[1,2,6,24,384]{4,3,2,1,0:T(8,128)}, f32[1,2,6,24,384]{4,3,2,1,0:T(8,128)}, ...) custom-call(f32[198,8,384]{2,1,0:T(8,128)} %get-tuple-element.20.ref, ...), custom_call_target="tpu_custom_call" | custom-call | tf_op jit(solution)/shard_map/pallas_call | solution.py:1281

commit v4 on v3

--- a/solution.py
+++ b/solution.py
@@ -429,6 +429,7 @@
         grad = dot_nt(s.low_g[...], s.w_down[layer, cols, :])
         grad = (grad * s.slope[layer, :, cols].astype(F32)).astype(BF16)
         s.slope[layer, :, cols] = grad
+        s.vec_grad[layer, 1:2, cols] = jnp.sum(fold_rows(grad.astype(F32)), 0, keepdims=True)
         half, first = number // per_half, (number % per_half) * 2
         down = dot_tn(s.act[layer, :, cols], s.low_g[...]).astype(BF16)
         up = dot_tn(grad, s.low_b[layer]).astype(BF16)
@@ -438,10 +439,6 @@
                 s.grads[half, g, odd, start : start + some, :] = value[n * some : (n + 1) * some]
 
     loop(FF // tile, unit_tile)
-
-
-def backward_up_sums(dm, layer, s):
-    s.vec_grad[layer, 1:2, :] = column_sums(dm, lambda rows: s.slope[layer, rows, :], FF)
 
 
 def backward_down(dm, layer, s):
@@ -507,8 +504,10 @@
 
 
 def backward_sums(dm, layer, s):
-    wide = 3 * HEADS * HD
-    s.vec_grad[layer, 0:1, :wide] = column_sums(dm, lambda rows: s.qkv[layer, rows, :], wide)
+    wide = HEADS * HD
+    for start in (0, 2 * wide):
+        cols = slice(start, start + wide)
+        s.vec_grad[layer, 0:1, cols] = column_sums(dm, lambda rows: s.qkv[layer, rows, cols], wide)
 
 
 def backward_project(dm, layer, s):
@@ -530,7 +529,6 @@
 BACKWARD = (
     ("start", backward_start),
     ("units", backward_units),
-    ("sums", backward_up_sums),
     ("down", backward_down),
     ("mid", backward_norm_b),
     ("out", backward_out),
@@ -1017,18 +1015,18 @@
     other_vec = net.copy(("vectors", 1, 0), 0, s.vec_own, s.vec_in, net.sibling())
     other_vec.start()
     prepare_codes(dm, slot_block, s)
+    gathers[0].spread(0)
     prepare_keep(dm, keep_mask, first, s)
+    gathers[0].spread_last()
+    gathers[0].cross(1)
     wait_all(tokens.load(hidden))
     load_tokens(dm, s.tok_in, s.hid)
     start_all(tokens.load(cotangent))
     other_vec.wait()
     s.vec[...] = s.vec_own[...] + s.vec_in[...]
-    gathers[0].spread(0)
-    gathers[0].spread_last()
-    for piece in range(1, depth):
+    for piece in range(2, depth):
         gathers[0].cross(piece)
-        if piece > 1:
-            gathers[0].spread(piece - 1)
+        gathers[0].spread(piece - 1)
     gathers[1].along_depth()
     gathers[0].spread(depth - 1)
     gathers[1].begin()

time: 126 us -> 125 us (level)
  no operation moved by 1% of the time
where the time goes in v4:
time: 125 us
  Pallas kernels  124 us (99%)
    pallas_call x1, Pallas kernels, run_step(): pl.pallas_call(functools.partial(step_kernel, dm, tuple(shapes)), out_sha...  119 us
    pallas_call x1, Pallas kernels, run_finish(): pl.pallas_call(functools.partial(finish_kernel, parts), out_shape=tuple((...  5.05 us

profile of v4, /device:TPU:0, one launch (start us, length us, event | category | flops | bytes accessed | tf_op | source)
XLA Modules:
  0.0 125.0 jit_solution(13909759334636019041)
XLA Ops:
  0.6 119.1 %shard_map.161 = (f32[198,8,384]{2,1,0:T(8,128)}, f32[198,8,384]{2,1,0:T(8,128)}, f32[1,2,6,24,384]{4,3,2,1,0:T(8,128)}, f32[1,6,2,384]{3,2,1,0:T(2,128)}) custom-call(f32[198,8,384]{2,1,0:T(8,128)} %bitcast.16, s32[8,198]{1,0:T(8,128)} %keep_far.1, f32[198,8,384]{2,1,0:T(8,128)} %bitcast.17, s32[2,384]{1,0:T(2,128)} %slots_far.1, ...), custom_call_target="tpu_custom_call" | custom-call | tf_op jit(solution)/shard_map/pallas_call | solution.py:1207
  119.8 5.1 %shard_map.162 = (f32[198,8,384]{2,1,0:T(8,128)}, f32[198,8,384]{2,1,0:T(8,128)}, f32[1,2,6,24,384]{4,3,2,1,0:T(8,128)}, f32[1,2,6,24,384]{4,3,2,1,0:T(8,128)}, ...) custom-call(f32[198,8,384]{2,1,0:T(8,128)} %get-tuple-element.20.ref, ...), custom_call_target="tpu_custom_call" | custom-call | tf_op jit(solution)/shard_map/pallas_call | solution.py:1279

commit v5 on v4

--- a/solution.py
+++ b/solution.py
@@ -407,15 +407,6 @@
     return jnp.sum(total, 0, keepdims=True)
 
 
-def column_sums(dm, read, cols):
-    def chunk(i, carry):
-        rows = pl.ds(pl.multiple_of(i * NORM_ROWS, NORM_ROWS), NORM_ROWS)
-        return carry + fold_rows(read(rows).astype(F32))
-
-    total = lax.fori_loop(0, dm.tokens // NORM_ROWS, chunk, jnp.zeros((8, cols), F32), unroll=True)
-    return jnp.sum(total, 0, keepdims=True)
-
-
 def backward_start(dm, layer, s):
     s.vec_grad[layer, 7:8, : dm.width] = low_and_sum(dm, s.hid, s.low_g)
 
@@ -499,15 +490,12 @@
 def backward_rows(dm, layer, s):
     wide = HEADS * HD
     for kind in range(3):
-        value = dot_tn(s.qkv[layer, :, kind * wide : (kind + 1) * wide], s.low_a[layer])
+        cols = slice(kind * wide, (kind + 1) * wide)
+        grad = s.qkv[layer, :, cols]
+        if kind != 1:
+            s.vec_grad[layer, 0:1, cols] = jnp.sum(fold_rows(grad.astype(F32)), 0, keepdims=True)
+        value = dot_tn(grad, s.low_a[layer])
         put_grads(dm, s, kind, value.astype(BF16))
-
-
-def backward_sums(dm, layer, s):
-    wide = HEADS * HD
-    for start in (0, 2 * wide):
-        cols = slice(start, start + wide)
-        s.vec_grad[layer, 0:1, cols] = column_sums(dm, lambda rows: s.qkv[layer, rows, cols], wide)
 
 
 def backward_project(dm, layer, s):
@@ -535,7 +523,6 @@
     ("attend", functools.partial(backward_attend, part=0)),
     ("attended", functools.partial(backward_attend, part=1)),
     ("rows", backward_rows),
-    ("more", backward_sums),
     ("project", backward_project),
     ("end", backward_norm_a),
 )

time: 125 us -> 125 us (level)
  no operation moved by 1% of the time
where the time goes in v5:
time: 125 us
  Pallas kernels  124 us (99%)
    pallas_call x1, Pallas kernels, run_step(): pl.pallas_call(functools.partial(step_kernel, dm, tuple(shapes)), out_sha...  119 us
    pallas_call x1, Pallas kernels, run_finish(): pl.pallas_call(functools.partial(finish_kernel, parts), out_shape=tuple((...  5.05 us

profile of v5, /device:TPU:0, one launch (start us, length us, event | category | flops | bytes accessed | tf_op | source)
XLA Modules:
  0.0 125.0 jit_solution(13277188584205535570)
XLA Ops:
  0.6 119.2 %shard_map.161 = (f32[198,8,384]{2,1,0:T(8,128)}, f32[198,8,384]{2,1,0:T(8,128)}, f32[1,2,6,24,384]{4,3,2,1,0:T(8,128)}, f32[1,6,2,384]{3,2,1,0:T(2,128)}) custom-call(f32[198,8,384]{2,1,0:T(8,128)} %bitcast.16, s32[8,198]{1,0:T(8,128)} %keep_far.1, f32[198,8,384]{2,1,0:T(8,128)} %bitcast.17, s32[2,384]{1,0:T(2,128)} %slots_far.1, ...), custom_call_target="tpu_custom_call" | custom-call | tf_op jit(solution)/shard_map/pallas_call | solution.py:1194
  119.8 5.1 %shard_map.162 = (f32[198,8,384]{2,1,0:T(8,128)}, f32[198,8,384]{2,1,0:T(8,128)}, f32[1,2,6,24,384]{4,3,2,1,0:T(8,128)}, f32[1,2,6,24,384]{4,3,2,1,0:T(8,128)}, ...) custom-call(f32[198,8,384]{2,1,0:T(8,128)} %get-tuple-element.20.ref, ...), custom_call_target="tpu_custom_call" | custom-call | tf_op jit(solution)/shard_map/pallas_call | solution.py:1266
